TPU v7x, 256 devices: a whole 4x4x8 slice. The times are simulated.
256 devices in a mesh: ctx: 64 (over x, z, core), head: 4 (over y).
Axes of the slice: x: 4, y: 4, z: 8, core: 2. Of those that a mesh axis runs over, the one named last changes fastest.
Arguments:
- prefix_query: bfloat16 [2048, 8192], P(('ctx', 'head')), may hold values from -7 to 7
- prefix_key: bfloat16 [2048, 1024], P(('ctx', 'head')), may hold values from -6 to 6
- prefix_value: bfloat16 [2048, 1024], P(('ctx', 'head')), may hold values from -6 to 6
- prefix_cotangent: bfloat16 [2048, 8192], P(('ctx', 'head')), may hold values from -6 to 6
- reply_query: bfloat16 [16384, 8192], P('ctx', 'head'), may hold values from -7 to 7
- reply_key: bfloat16 [16384, 1024], P('ctx', 'head'), may hold values from -6 to 6
- reply_value: bfloat16 [16384, 1024], P('ctx', 'head'), may hold values from -6 to 6
- reply_cotangent: bfloat16 [16384, 8192], P('ctx', 'head'), may hold values from -6 to 6
- parent: int32 [64], P('ctx'), may hold values from 0 to 1
- lengths: int32 [64], P('ctx'), may hold values from 1 to 256, 10240 in all
Outputs:
- prefix_output: bfloat16 [2048, 8192], P(('ctx', 'head'))
- prefix_query_gradient: bfloat16 [2048, 8192], P(('ctx', 'head'))
- prefix_key_gradient: bfloat16 [2048, 1024], P(('ctx', 'head'))
- prefix_value_gradient: bfloat16 [2048, 1024], P(('ctx', 'head'))
- reply_output: bfloat16 [16384, 8192], P('ctx', 'head')
- reply_query_gradient: bfloat16 [16384, 8192], P('ctx', 'head')
- reply_key_gradient: bfloat16 [16384, 1024], P('ctx', 'head')
- reply_value_gradient: bfloat16 [16384, 1024], P('ctx', 'head')
Inputs may be any that keep to these rules, and one draw needn't show every extreme that they name: The lengths sum to 10240 and the longest is exactly 256.
All inputs are finite; a program needn't handle non-finite values. No bound on the sum of `lengths` on one device may be relied on, other than what follows from the above.
Results may differ from a plain program's by a relative error of at most 0.035.
Values may be sent and summed in bfloat16 or wider, within the bound.
No kernel may reach another device: no remote copies, remote signals or barrier semaphores. Data moves between devices by JAX's collectives and lax.ppermute only.
A program may use at most 128 MiB of HBM per device.

v0:
```python
from functools import reduce
import math

import jax
import jax.numpy as jnp
from jax import lax
from jax.sharding import PartitionSpec as P

HD = 128
GROUP = 8
PROMPTS = 2


def head_ranges(kv_local, block_heads):
    ranges_out = []
    for head_kv in range(kv_local):
        for first_head in range(head_kv * GROUP, (head_kv + 1) * GROUP, block_heads):
            ranges_out.append((head_kv, first_head, first_head + block_heads))
    return ranges_out


def forward_blocks(
    query, cotangent, key_set, value_set, visible, live_float, block_heads, score_scale
):
    row_count = query.shape[0]
    kv_local = key_set.shape[1] // HD
    query_heads = query.reshape(row_count, kv_local * GROUP, HD)
    cotan_heads = cotangent.reshape(row_count, kv_local * GROUP, HD)
    output_parts = []
    log_parts = []
    dot_parts = []
    for head_kv, first_head, last_head in head_ranges(kv_local, block_heads):
        key_head = key_set[:, head_kv * HD : (head_kv + 1) * HD]
        value_head = value_set[:, head_kv * HD : (head_kv + 1) * HD]
        query_block = query_heads[:, first_head:last_head]
        scores = (
            jnp.einsum("rnd,kd->nrk", query_block, key_head, preferred_element_type=jnp.float32)
            * score_scale
        )
        scores = jnp.where(visible[None], scores, -jnp.inf)
        row_max = jnp.max(scores, axis=2, keepdims=True)
        log_total = row_max + jnp.log(jnp.sum(jnp.exp(scores - row_max), axis=2, keepdims=True))
        weights_half = (jnp.exp(scores - log_total) * live_float[None, :, None]).astype(
            jnp.bfloat16
        )
        output_block = jnp.einsum(
            "nrk,kd->rnd", weights_half, value_head, preferred_element_type=jnp.float32
        ).astype(jnp.bfloat16)
        dot_parts.append(
            jnp.einsum(
                "rnd,rnd->nr",
                output_block,
                cotan_heads[:, first_head:last_head],
                preferred_element_type=jnp.float32,
            )[:, :, None]
        )
        output_parts.append(output_block)
        log_parts.append(log_total)
    output = jnp.concatenate(output_parts, axis=1).reshape(row_count, -1)
    return (output, log_parts, dot_parts)


def backward_blocks(
    query,
    cotangent,
    key_set,
    value_set,
    visible,
    live_float,
    log_parts,
    dot_parts,
    block_heads,
    score_scale,
):
    row_count = query.shape[0]
    kv_local = key_set.shape[1] // HD
    query_heads = query.reshape(row_count, kv_local * GROUP, HD)
    cotan_heads = cotangent.reshape(row_count, kv_local * GROUP, HD)
    query_parts = []
    key_lists = [[] for head_kv in range(kv_local)]
    value_lists = [[] for head_kv in range(kv_local)]
    for position, (head_kv, first_head, last_head) in enumerate(head_ranges(kv_local, block_heads)):
        key_head = key_set[:, head_kv * HD : (head_kv + 1) * HD]
        value_head = value_set[:, head_kv * HD : (head_kv + 1) * HD]
        query_block = query_heads[:, first_head:last_head]
        cotan_block = cotan_heads[:, first_head:last_head]
        scores = (
            jnp.einsum("rnd,kd->nrk", query_block, key_head, preferred_element_type=jnp.float32)
            * score_scale
        )
        scores = jnp.where(visible[None], scores, -jnp.inf)
        weights = jnp.exp(scores - log_parts[position]) * live_float[None, :, None]
        weights_half = weights.astype(jnp.bfloat16)
        weight_grad = jnp.einsum(
            "rnd,kd->nrk", cotan_block, value_head, preferred_element_type=jnp.float32
        )
        score_grad = (weights * (weight_grad - dot_parts[position])).astype(jnp.bfloat16)
        query_parts.append(
            jnp.einsum("nrk,kd->rnd", score_grad, key_head, preferred_element_type=jnp.float32)
            * score_scale
        )
        key_lists[head_kv].append(
            jnp.einsum("nrk,rnd->kd", score_grad, query_block, preferred_element_type=jnp.float32)
            * score_scale
        )
        value_lists[head_kv].append(
            jnp.einsum("nrk,rnd->kd", weights_half, cotan_block, preferred_element_type=jnp.float32)
        )
    query_grad = jnp.concatenate(query_parts, axis=1).reshape(row_count, -1)
    key_grad = jnp.concatenate([reduce(jnp.add, parts_list) for parts_list in key_lists], axis=1)
    value_grad = jnp.concatenate(
        [reduce(jnp.add, parts_list) for parts_list in value_lists], axis=1
    )
    return (query_grad, key_grad, value_grad)


def shards(
    prefix_query,
    prefix_key,
    prefix_value,
    prefix_cotangent,
    reply_query,
    reply_key,
    reply_value,
    reply_cotangent,
    parent,
    lengths,
):
    score_scale = 1.0 / math.sqrt(HD)
    prefix_heads = GROUP
    reply_heads = GROUP // 2
    own_query, own_cotan, own_key, own_value = (
        lax.all_to_all(prefix_query, "head", split_axis=1, concat_axis=0, tiled=True),
        lax.all_to_all(prefix_cotangent, "head", split_axis=1, concat_axis=0, tiled=True),
        lax.all_to_all(prefix_key, "head", split_axis=1, concat_axis=0, tiled=True),
        lax.all_to_all(prefix_value, "head", split_axis=1, concat_axis=0, tiled=True),
    )
    every_key, every_value = (
        lax.all_gather(own_key, "ctx", axis=0, tiled=True),
        lax.all_gather(own_value, "ctx", axis=0, tiled=True),
    )
    owned_rows = own_key.shape[0]
    prefix_len = every_key.shape[0] // PROMPTS
    first_row = lax.axis_index("ctx") * owned_rows
    own_prompt = first_row // prefix_len
    query_pos = first_row - own_prompt * prefix_len + jnp.arange(owned_rows, dtype=jnp.int32)
    key_pos = jnp.arange(prefix_len, dtype=jnp.int32)
    prefix_visible = query_pos[:, None] >= key_pos[None, :]
    prompt_keys = lax.dynamic_slice_in_dim(every_key, own_prompt * prefix_len, prefix_len, 0)
    prompt_values = lax.dynamic_slice_in_dim(every_value, own_prompt * prefix_len, prefix_len, 0)
    prefix_live = jnp.ones((owned_rows,), jnp.float32)
    prefix_output, prefix_logs, prefix_dots = forward_blocks(
        own_query,
        own_cotan,
        prompt_keys,
        prompt_values,
        prefix_visible,
        prefix_live,
        prefix_heads,
        score_scale,
    )
    source = parent[0]
    parent_keys = lax.dynamic_slice_in_dim(every_key, source * prefix_len, prefix_len, 0)
    parent_values = lax.dynamic_slice_in_dim(every_value, source * prefix_len, prefix_len, 0)
    reply_slots = reply_query.shape[0]
    slot_index = jnp.arange(reply_slots, dtype=jnp.int32)
    own_visible = slot_index[:, None] >= slot_index[None, :]
    parent_visible = jnp.ones((reply_slots, prefix_len), jnp.bool_)
    reply_live = (slot_index < lengths[0]).astype(jnp.float32)
    joint_keys = jnp.concatenate([parent_keys, reply_key], axis=0)
    joint_values = jnp.concatenate([parent_values, reply_value], axis=0)
    joint_visible = jnp.concatenate([parent_visible, own_visible], axis=1)
    reply_output, reply_logs, reply_dots = forward_blocks(
        reply_query,
        reply_cotangent,
        joint_keys,
        joint_values,
        joint_visible,
        reply_live,
        reply_heads,
        score_scale,
    )
    self_grads = backward_blocks(
        own_query,
        own_cotan,
        prompt_keys,
        prompt_values,
        prefix_visible,
        prefix_live,
        prefix_logs,
        prefix_dots,
        prefix_heads,
        score_scale,
    )
    joint_grads = backward_blocks(
        reply_query,
        reply_cotangent,
        joint_keys,
        joint_values,
        joint_visible,
        reply_live,
        reply_logs,
        reply_dots,
        reply_heads,
        score_scale,
    )
    prefix_qgrad = self_grads[0]
    reply_qgrad = joint_grads[0]
    reply_kgrad = joint_grads[1][prefix_len:]
    reply_vgrad = joint_grads[2][prefix_len:]
    key_pieces = []
    value_pieces = []
    for prompt in range(PROMPTS):
        own_flag = (own_prompt == prompt).astype(jnp.float32)
        parent_flag = (source == prompt).astype(jnp.float32)
        key_pieces.append(own_flag * self_grads[1] + parent_flag * joint_grads[1][:prefix_len])
        value_pieces.append(own_flag * self_grads[2] + parent_flag * joint_grads[2][:prefix_len])
    key_sum, value_sum = (
        lax.psum_scatter(
            jnp.concatenate(key_pieces, axis=0), "ctx", scatter_dimension=0, tiled=True
        ),
        lax.psum_scatter(
            jnp.concatenate(value_pieces, axis=0), "ctx", scatter_dimension=0, tiled=True
        ),
    )
    returned = (
        lax.all_to_all(prefix_output, "head", split_axis=0, concat_axis=1, tiled=True),
        lax.all_to_all(
            prefix_qgrad.astype(jnp.bfloat16), "head", split_axis=0, concat_axis=1, tiled=True
        ),
        lax.all_to_all(
            key_sum.astype(jnp.bfloat16), "head", split_axis=0, concat_axis=1, tiled=True
        ),
        lax.all_to_all(
            value_sum.astype(jnp.bfloat16), "head", split_axis=0, concat_axis=1, tiled=True
        ),
    )
    return (
        returned[0],
        returned[1],
        returned[2],
        returned[3],
        reply_output,
        reply_qgrad.astype(jnp.bfloat16),
        reply_kgrad.astype(jnp.bfloat16),
        reply_vgrad.astype(jnp.bfloat16),
    )


def solution(mesh):
    return jax.shard_map(
        shards,
        mesh=mesh,
        in_specs=(
            P(("ctx", "head"), None),
            P(("ctx", "head"), None),
            P(("ctx", "head"), None),
            P(("ctx", "head"), None),
            P("ctx", "head"),
            P("ctx", "head"),
            P("ctx", "head"),
            P("ctx", "head"),
            P("ctx"),
            P("ctx"),
        ),
        out_specs=(
            P(("ctx", "head"), None),
            P(("ctx", "head"), None),
            P(("ctx", "head"), None),
            P(("ctx", "head"), None),
            P("ctx", "head"),
            P("ctx", "head"),
            P("ctx", "head"),
            P("ctx", "head"),
        ),
        check_vma=False,
    )
```

profile of v0, /device:TPU:1, one launch (start us, length us, event | category | flops | bytes accessed | tf_op | source)
XLA Modules:
  0.0 539.0 jit_solution(11525147458680154409)
XLA Ops:
  7.2 9.3 %all_to_all.143 = bf16[8,4,256]{2,0,1:T(8,128)(2,1)} all-to-all(bf16[8,4,256]{2,0,1:T(8,128)(2,1)} %bitcast.302), channel_id=1, replica_groups=mesh['ctx'=64,'head'=4] {'head'}, dimensions={1} | all-to-all | bytes 32768 | tf_op jit(solution)/shard_map/all_to_all | solution.py:135
  16.6 8.1 %all_to_all.144 = bf16[8,4,256]{2,0,1:T(8,128)(2,1)} all-to-all(bf16[8,4,256]{2,0,1:T(8,128)(2,1)} %bitcast.303), channel_id=1, replica_groups=mesh['ctx'=64,'head'=4] {'head'}, dimensions={1} | all-to-all | bytes 32768 | tf_op jit(solution)/shard_map/all_to_all | solution.py:136
  24.8 3.3 all-to-all-start.2
  36.0 4.2 all-to-all-start.4
  40.2 4.8 all-to-all-done.4
  45.1 50.8 %all-gather.5.cloned.1.call-done = bf16[2048,256]{1,0:T(8,128)(2,1)} async-done(((bf16[32,256]{1,0:T(8,128)(2,1)}), bf16[2048,256]{1,0:T(8,128)(2,1)}) %all-gather.5.cloned.1.call-update) | async-done | bytes 1048592 | tf_op jit(solution)/shard_map/all_gather | solution.py:139
  95.9 76.9 %all-gather.3.cloned.1.call-done = bf16[2048,256]{1,0:T(8,128)(2,1)} async-done(((bf16[32,256]{1,0:T(8,128)(2,1)}), bf16[2048,256]{1,0:T(8,128)(2,1)}) %all-gather.3.cloned.1.call-update) | async-done | bytes 1048592 | tf_op jit(solution)/shard_map/all_gather | solution.py:140
  175.9 4.2 fusion.104
  180.1 3.2 fusion.101
  183.4 3.3 fusion.102
  196.0 2.0 convolution_bitcast_fusion.3
  202.2 5.4 %fusion.7 = bf16[4,256,1280]{1,2,0:T(8,128)(2,1)} fusion(f32[4,256,1280]{1,2,0:T(8,128)} %copy-done, bf16[1280,128,1]{1,0,2:T(8,128)(2,1)S(1)} %get-tuple-element.40, f32[4,256]{1,0:T(4,128)S(1)} %multiply_reduce_fusion.3, f32[256]{0:T(256)S(1)} %compare_convert_fusion, f32[4,256]{1,0:T(4,128)S(1)} %log_add_fusion.3, bf16[256,16,128]{0,2,1:T(8,128)(2,1)S(1)} %bitcast.267), kind=kOutput, calls=%fused_computation.14 | convolution fusion | flops 342097920 | bytes 8463360 | tf_op jit(solution)/shard_map/rnd,kd->nrk/dot_general | solution.py:94
  208.4 2.0 bitcast_convert_fusion.2
  213.3 3.2 exponential_reduce_fusion.1
  217.2 4.5 convolution_bitcast_fusion.1
  221.7 4.4 bitcast_convert_fusion.1
  227.1 3.3 exponential_reduce_fusion
  231.1 4.6 bitcast_convert_fusion
  239.3 3.0 copy.244
  246.4 2.0 copy.213
  249.9 2.1 convolution_bitcast_fusion.7
  252.0 3.9 fusion.3
  265.4 3.0 copy.242
  272.9 4.0 all-to-all-start.3
  276.9 2.6 fusion.37
  284.5 4.2 all-to-all-start.5
  288.8 86.3 %reduce-scatter.9.cloned.1.call-done = f32[32,256]{1,0:T(8,128)} async-done(((f32[2048,256]{1,0:T(8,128)}), f32[32,256]{1,0:T(8,128)}) %reduce-scatter.9.cloned.1.call-update) | async-done | bytes 32784 | tf_op jit(solution)/shard_map/reduce_scatter | solution.py:222
  376.5 4.1 all-to-all-start.7
  380.5 137.9 %reduce-scatter.7.cloned.1.call-done = f32[32,256]{1,0:T(8,128)} async-done(((f32[2048,256]{1,0:T(8,128)}), f32[32,256]{1,0:T(8,128)}) %reduce-scatter.7.cloned.1.call-update) | async-done | bytes 32784 | tf_op jit(solution)/shard_map/reduce_scatter | solution.py:219
  519.8 4.1 all-to-all-start.6
  524.7 2.3 copy.161
  526.9 2.3 copy.160
  (201 shorter events, 63.7 us)
Async XLA Ops:
  7.2 88.7 %all-gather.5.cloned.1.call-start = ((), (), s32[]{:S(2)}) async-start(), calls=%async_computation.11 | async-start | bytes 1064960 | tf_op jit(solution)/shard_map/all_gather | solution.py:139
  16.6 156.2 %all-gather.3.cloned.1.call-start = ((), (), s32[]{:S(2)}) async-start(), calls=%async_computation.10 | async-start | bytes 1064960 | tf_op jit(solution)/shard_map/all_gather | solution.py:140
  24.8 11.2 %all-to-all-start.2 = ((bf16[8,4,2048]{2,0,1:T(8,128)(2,1)}), bf16[8,4,2048]{2,0,1:T(8,128)(2,1)S(1)}, u32[]{:S(2)}, u32[]{:S(2)}) async-start(bf16[8,4,2048]{2,0,1:T(8,128)(2,1)} %bitcast.296), calls=%async_computation.2 | async-start | bytes 262144 | tf_op jit(solution)/shard_map/all_to_all | solution.py:133
  31.0 152.4 %copy-start.10 = (bf16[256,2048]{0,1:T(8,128)(2,1)}, bf16[256,2048]{0,1:T(8,128)(2,1)S(1)}, u32[]{:S(2)}) copy-start(bf16[256,2048]{0,1:T(8,128)(2,1)S(1)} %copy.116) | copy-start | bytes 3145732
  32.8 202.9 %copy-start.6 = (bf16[256,2048]{0,1:T(8,128)(2,1)}, bf16[256,2048]{0,1:T(8,128)(2,1)S(1)}, u32[]{:S(2)}) copy-start(bf16[256,2048]{0,1:T(8,128)(2,1)S(1)} %copy.118) | copy-start | bytes 3145732
  36.0 9.0 %all-to-all-start.4 = ((bf16[8,4,2048]{2,0,1:T(8,128)(2,1)}), bf16[8,4,2048]{2,0,1:T(8,128)(2,1)S(1)}, u32[]{:S(2)}, u32[]{:S(2)}) async-start(bf16[8,4,2048]{2,0,1:T(8,128)(2,1)} %bitcast.297), calls=%async_computation.4 | async-start | bytes 262144 | tf_op jit(solution)/shard_map/all_to_all | solution.py:134
  40.2 334.9 %reduce-scatter.9.cloned.1.call-start = ((), (), s32[]{:S(2)}) async-start(), calls=%async_computation.13 | async-start | bytes 2129920 | tf_op jit(solution)/shard_map/reduce_scatter | solution.py:222
  174.9 8.4 %copy-start.14 = (bf16[1280,128,1]{1,0,2:T(8,128)(2,1)}, bf16[1280,128,1]{1,0,2:T(8,128)(2,1)S(1)}, u32[]{:S(2)}) copy-start(bf16[1280,128,1]{1,0,2:T(8,128)(2,1)S(1)} %get-tuple-element.43) | copy-start | bytes 983044
  175.9 22.1 %copy-start = (f32[4,256,1280]{1,2,0:T(8,128)}, f32[4,256,1280]{1,2,0:T(8,128)S(1)}, u32[]{:S(2)}) copy-start(f32[4,256,1280]{1,2,0:T(8,128)S(1)} %get-tuple-element.65) | copy-start | bytes 15728644
  180.1 6.5 %copy-start.30 = (bf16[2048,256]{1,0:T(8,128)(2,1)S(1)}, bf16[2048,256]{1,0:T(8,128)(2,1)}, u32[]{:S(2)}) copy-start(bf16[2048,256]{1,0:T(8,128)(2,1)} %all-gather.5.cloned.1.call-done) | copy-start | bytes 3145732
  183.3 30.0 %copy-start.39 = (f32[4,256]{1,0:T(4,128)}, f32[4,256]{1,0:T(4,128)S(1)}, u32[]{:S(2)}) copy-start(f32[4,256]{1,0:T(4,128)S(1)} %get-tuple-element.56) | copy-start | bytes 12292
  186.7 40.4 %copy-start.38 = (f32[4,256]{1,0:T(4,128)}, f32[4,256]{1,0:T(4,128)S(1)}, u32[]{:S(2)}) copy-start(f32[4,256]{1,0:T(4,128)S(1)} %get-tuple-element.60) | copy-start | bytes 12292
  196.0 55.9 %copy-start.12 = (bf16[1280,128,1]{1,0,2:T(8,128)(2,1)}, bf16[1280,128,1]{1,0,2:T(8,128)(2,1)S(1)}, u32[]{:S(2)}) copy-start(bf16[1280,128,1]{1,0,2:T(8,128)(2,1)S(1)} %get-tuple-element.41) | copy-start | bytes 983044
  199.9 7.8 %slice-start.4 = ((s8[5242880]{0:T(1024)(128)(4,1)}), s8[1048576]{0:T(1024)(128)(4,1)S(1)}, s32[]{:S(2)}) async-start(s8[5242880]{0:T(1024)(128)(4,1)} %bitcast.261), calls=%async_computation.18 | async-start | bytes 2097152
  200.9 6.8 %copy-start.40 = (f32[4,256]{1,0:T(4,128)S(1)}, f32[4,256]{1,0:T(4,128)}, u32[]{:S(2)}) copy-start(f32[4,256]{1,0:T(4,128)} %get-tuple-element.68) | copy-start | bytes 12292
  221.7 14.1 %slice-start = ((s8[5242880]{0:T(1024)(128)(4,1)}), s8[1048576]{0:T(1024)(128)(4,1)S(1)}, s32[]{:S(2)}) async-start(s8[5242880]{0:T(1024)(128)(4,1)} %bitcast.257), calls=%async_computation.14 | async-start | bytes 2097152
  227.1 8.7 %slice-start.1 = ((s8[5242880]{0:T(1024)(128)(4,1)}), s8[4194304]{0:T(1024)(128)(4,1)S(1)}, s32[]{:S(2)}) async-start(s8[5242880]{0:T(1024)(128)(4,1)} %bitcast.257), calls=%async_computation.15 | async-start | bytes 8388608
  227.1 8.7 %copy-start.22 = (f32[1280,128]{0,1:T(8,128)S(1)}, f32[1280,128]{0,1:T(8,128)}, u32[]{:S(2)}) copy-start(f32[1280,128]{0,1:T(8,128)} %convolution_bitcast_fusion.1) | copy-start | bytes 1966084
  231.1 5.8 %copy-start.17 = (f32[1280,128]{0,1:T(8,128)S(1)}, f32[1280,128]{0,1:T(8,128)}, u32[]{:S(2)}) copy-start(f32[1280,128]{0,1:T(8,128)} %fusion.13) | copy-start | bytes 1966084
  231.1 5.8 %copy-start.26 = (f32[1024,128]{0,1:T(8,128)S(1)}, f32[1024,128]{0,1:T(8,128)}, u32[]{:S(2)}) copy-start(f32[1024,128]{0,1:T(8,128)} %convolution_bitcast_fusion.10) | copy-start | bytes 1572868
  231.1 5.8 %copy-start.27 = (f32[1024,128]{0,1:T(8,128)S(1)}, f32[1024,128]{0,1:T(8,128)}, u32[]{:S(2)}) copy-start(f32[1024,128]{0,1:T(8,128)} %convolution_bitcast_fusion.11) | copy-start | bytes 1572868
  239.3 10.6 %copy-start.3 = (bf16[4,256,1280]{1,2,0:T(8,128)(2,1)S(1)}, bf16[4,256,1280]{1,2,0:T(8,128)(2,1)}, u32[]{:S(2)}) copy-start(bf16[4,256,1280]{1,2,0:T(8,128)(2,1)} %fusion.7) | copy-start | bytes 7864324
  242.4 276.1 %reduce-scatter.7.cloned.1.call-start = ((), (), s32[]{:S(2)}) async-start(), calls=%async_computation.12 | async-start | bytes 2129920 | tf_op jit(solution)/shard_map/reduce_scatter | solution.py:219
  246.4 5.6 %copy-start.42 = (f32[4,256]{1,0:T(4,128)S(1)}, f32[4,256]{1,0:T(4,128)}, u32[]{:S(2)}) copy-start(f32[4,256]{1,0:T(4,128)} %multiply_reduce_fusion.1) | copy-start | bytes 12292
  249.9 7.1 %slice-start.6 = ((s8[5242880]{0:T(1024)(128)(4,1)}), s8[4194304]{0:T(1024)(128)(4,1)S(1)}, s32[]{:S(2)}) async-start(s8[5242880]{0:T(1024)(128)(4,1)} %bitcast.263), calls=%async_computation.20 | async-start | bytes 8388608
  265.4 6.7 %copy-start.35 = (bf16[128,8,32]{0,2,1:T(8,128)(2,1)S(1)}, bf16[128,8,32]{0,2,1:T(8,128)(2,1)}, u32[]{:S(2)}) copy-start(bf16[128,8,32]{0,2,1:T(8,128)(2,1)} %get-tuple-element.53) | copy-start | bytes 196612
  265.4 6.7 %copy-start.36 = (bf16[128,8,32]{0,2,1:T(8,128)(2,1)S(1)}, bf16[128,8,32]{0,2,1:T(8,128)(2,1)}, u32[]{:S(2)}) copy-start(bf16[128,8,32]{0,2,1:T(8,128)(2,1)} %get-tuple-element.55) | copy-start | bytes 196612
  272.9 11.7 %all-to-all-start.3 = ((bf16[4,8,2048]{2,1,0:T(8,128)(2,1)}), bf16[4,8,2048]{2,1,0:T(8,128)(2,1)S(1)}, u32[]{:S(2)}, u32[]{:S(2)}) async-start(bf16[4,8,2048]{2,1,0:T(8,128)(2,1)} %all_to_all.117), calls=%async_computation.3 | async-start | bytes 262144 | tf_op jit(solution)/shard_map/all_to_all | solution.py:227
  281.7 242.2 %copy-start.9 = (f32[1280,128]{0,1:T(8,128)S(1)}, f32[1280,128]{0,1:T(8,128)}, u32[]{:S(2)}) copy-start(f32[1280,128]{0,1:T(8,128)} %copy-done.8) | copy-start | bytes 1966084
  284.5 91.9 %all-to-all-start.5 = ((bf16[4,8,2048]{2,1,0:T(8,128)(2,1)}), bf16[4,8,2048]{2,1,0:T(8,128)(2,1)S(1)}, u32[]{:S(2)}, u32[]{:S(2)}) async-start(bf16[4,8,2048]{2,1,0:T(8,128)(2,1)} %convert_element_type.128), calls=%async_computation.5 | async-start | bytes 262144 | tf_op jit(solution)/shard_map/all_to_all | solution.py:228
  376.5 143.4 %all-to-all-start.7 = ((bf16[4,8,256]{2,1,0:T(8,128)(2,1)}), bf16[4,8,256]{2,1,0:T(8,128)(2,1)S(1)}, u32[]{:S(2)}, u32[]{:S(2)}) async-start(bf16[4,8,256]{2,1,0:T(8,128)(2,1)} %convert_bitcast_fusion), calls=%async_computation.7 | async-start | bytes 32768 | tf_op jit(solution)/shard_map/all_to_all | solution.py:234
  519.8 10.1 %all-to-all-start.6 = ((bf16[4,8,256]{2,1,0:T(8,128)(2,1)}), bf16[4,8,256]{2,1,0:T(8,128)(2,1)S(1)}, u32[]{:S(2)}, u32[]{:S(2)}) async-start(bf16[4,8,256]{2,1,0:T(8,128)(2,1)} %convert_bitcast_fusion.1), calls=%async_computation.6 | async-start | bytes 32768 | tf_op jit(solution)/shard_map/all_to_all | solution.py:231
  (29 other events, 97.2 us)
Sparse Core Ops, SparseCore 0:
  16.7 79.1 all-gather.4
  98.7 74.0 all-gather.2
  242.5 132.5 reduce-scatter.8
  379.5 138.8 reduce-scatter.6
where the time goes:
time: 546 us; the launch traced here: 539 us
  waiting for transfers between devices  357 us (65%)
  matrix products  67 us (12%)
  local copies, waits for them, and re-layouts  31.4 us (6%)
  other arithmetic  26.2 us (5%)
  starting transfers between devices  24.3 us (4%)
  blocking collectives  17.5 us (3%)
  between operations  15.9 us (3%)
    reduce_scatter x1, waiting for transfers between devices, shards(): lax.psum_scatter(jnp.concatenate(key_pieces, axis=0), 'ctx', scatter_dime...  138 us
    reduce_scatter x1, waiting for transfers between devices, shards(): lax.psum_scatter(jnp.concatenate(value_pieces, axis=0), 'ctx', scatter_di...  86.3 us
    all_gather x1, waiting for transfers between devices, shards(): lax.all_gather(own_value, 'ctx', axis=0, tiled=True)  76.9 us
    all_gather x1, waiting for transfers between devices, shards(): lax.all_gather(own_key, 'ctx', axis=0, tiled=True)  50.8 us
    unnamed x125, local copies, waits for them, and re-layouts  28.5 us
    dot_general x6, matrix products, forward_blocks(): jnp.einsum('nrk,kd->rnd', weights_half, value_head, preferred_element_typ...  14.8 us
    dot_general x6, matrix products, backward_blocks(): jnp.einsum('rnd,kd->nrk', cotan_block, value_head, preferred_element_type...  12.6 us
    dot_general x6, matrix products, backward_blocks(): jnp.einsum('nrk,rnd->kd', weights_half, cotan_block, preferred_element_ty...  11.9 us
  transfers between devices with their start and end apart: 10, of which 5 were waited for; matrix products, arithmetic and copies ran while one was open for 9% of the time, Pallas kernels for 0%

commit v1 on v0

v1 whole, which is shorter than its diff:
```python
import functools
import math

import jax
import jax.numpy as jnp
from jax import lax
from jax.experimental import pallas as pl
from jax.experimental.pallas import tpu as pltpu
from jax.sharding import Mesh, PartitionSpec as P
HD=128; GROUP=8; LEN=1024; SLOTS=256; ROWS=64; M=ROWS*GROUP
SCALE=1.0/math.sqrt(HD); LOG2E=math.log2(math.e)
NT=(((1,),(1,)),((),())); NN=(((1,),(0,)),((),()))
def dot(a,b,dims=NN): return lax.dot_general(a,b,dims,preferred_element_type=jnp.float32)
def stack(x): return jnp.concatenate([x[:,h*HD:(h+1)*HD] for h in range(GROUP)],axis=0)
def unstack(x): return jnp.concatenate([x[h*ROWS:(h+1)*ROWS] for h in range(GROUP)],axis=1)
def tr(x): return x.astype(jnp.float32).T.astype(jnp.bfloat16)

def pieces(q,do,parts,live):
    raw=[]
    for key,val,vis in parts:
        s=dot(q,key,NT)
        if vis is not None: s=jnp.where(vis,s,-1e30)
        raw.append(s)
    m=functools.reduce(jnp.maximum,[jnp.max(s,axis=1,keepdims=True) for s in raw])
    c=SCALE*LOG2E
    mc=m*c
    w=[jnp.exp2(s*c-mc) for s in raw]
    wh=[x.astype(jnp.bfloat16) for x in w]
    oe=functools.reduce(jnp.add,[dot(x,val) for x,(key,val,vis) in zip(wh,parts)])
    inv=1.0/oe[:,HD:]
    if live is not None: inv=inv*live
    o=(oe[:,:HD]*inv).astype(jnp.bfloat16)
    dof=do.astype(jnp.float32)
    dos=dof*inv
    rd=jnp.sum(o.astype(jnp.float32)*dos,axis=1,keepdims=True)
    hi=(-rd).astype(jnp.bfloat16).astype(jnp.float32)
    lo=-rd-hi
    lane=lax.broadcasted_iota(jnp.int32,(M,HD),1)
    ext=jnp.where(lane==0,hi,jnp.where(lane==1,lo,0.0)).astype(jnp.bfloat16)
    dob=dos.astype(jnp.bfloat16)
    doe=jnp.concatenate([dob,ext],axis=1)
    qT=tr(q); doT=dos.T.astype(jnp.bfloat16)
    dq=None; grads=[]
    for x,xh,(key,val,vis) in zip(w,wh,parts):
        dp=dot(doe,val,NT)
        ds=(x*dp).astype(jnp.bfloat16)
        t=dot(ds,key); dq=t if dq is None else dq+t
        grads.append((dot(qT,ds),dot(doT,xh)))
    return o,(dq*SCALE).astype(jnp.bfloat16),grads

def kernel(info,qa,da,qb,db,qp,dp_,k,v,ka,va,kb,vb,
           oa,ga,ob,gb,op,gp,kvg,owna,ownb, kT,vT,okT,ovT):
    u=pl.program_id(0)
    @pl.when(u==0)
    def _():
        kT[...]=jnp.zeros_like(kT); vT[...]=jnp.zeros_like(vT)
    r=u//4; b=u%4
    ones=lambda n: jnp.ones((n,HD),jnp.bfloat16)
    def reply(slot,q_ref,d_ref,ko,vo,o_ref,g_ref,own_ref):
        length=info[2+slot]; source=info[slot]
        @pl.when(b==0)
        def _():
            okT[...]=jnp.zeros_like(okT); ovT[...]=jnp.zeros_like(ovT)
        alive=b*ROWS<length
        @pl.when(jnp.logical_not(alive))
        def _():
            o_ref[...]=jnp.zeros_like(o_ref); g_ref[...]=jnp.zeros_like(g_ref)
        @pl.when(alive)
        def _():
            q=stack(q_ref[...]); d=stack(d_ref[...])
            off=pl.multiple_of(source*LEN,LEN)
            key=k[pl.ds(off,LEN),:]; val=jnp.concatenate([v[pl.ds(off,LEN),:],ones(LEN)],axis=1)
            valo=jnp.concatenate([vo[...],ones(SLOTS)],axis=1)
            row=b*ROWS+lax.broadcasted_iota(jnp.int32,(M,1),0)%ROWS
            vis=row>=lax.broadcasted_iota(jnp.int32,(M,SLOTS),1)
            live=(row<length).astype(jnp.float32)
            o,dq,gr=pieces(q,d,[(key,val,None),(ko[...],valo,vis)],live)
            o_ref[...]=unstack(o); g_ref[...]=unstack(dq)
            kT[:,pl.ds(off,LEN)]+=gr[0][0]; vT[:,pl.ds(off,LEN)]+=gr[0][1]
            okT[...]+=gr[1][0]; ovT[...]+=gr[1][1]
        @pl.when(b==3)
        def _():
            own_ref[:,:HD]=(okT[...]*SCALE).T.astype(jnp.bfloat16)
            own_ref[:,HD:]=ovT[...].T.astype(jnp.bfloat16)
    @pl.when(r==0)
    def _(): reply(0,qa,da,ka,va,oa,ga,owna)
    @pl.when(r==1)
    def _(): reply(1,qb,db,kb,vb,ob,gb,ownb)
    @pl.when(u==8)
    def _():
        q=stack(qp[...]); d=stack(dp_[...])
        off=pl.multiple_of(info[5]*LEN,LEN)
        key=k[pl.ds(off,LEN),:]; val=jnp.concatenate([v[pl.ds(off,LEN),:],ones(LEN)],axis=1)
        row=info[6]+lax.broadcasted_iota(jnp.int32,(M,1),0)%ROWS
        vis=row>=lax.broadcasted_iota(jnp.int32,(M,LEN),1)
        o,dq,gr=pieces(q,d,[(key,val,vis)],None)
        op[...]=unstack(o); gp[...]=unstack(dq)
        kT[:,pl.ds(off,LEN)]+=gr[0][0]; vT[:,pl.ds(off,LEN)]+=gr[0][1]
        kvg[:,:HD]=(kT[...]*SCALE).T.astype(jnp.bfloat16)
        kvg[:,HD:]=vT[...].T.astype(jnp.bfloat16)

def call(info,qa,da,qb,db,qp,dp_,k,v,ka,va,kb,vb):
    bf=jnp.bfloat16; G=GROUP*HD
    ia=lambda u,s:(jnp.minimum(u,3),s[4]); ib=lambda u,s:(jnp.clip(u-4,0,3),0); z=lambda u,s:(0,0)
    full=lambda a: pl.BlockSpec(a.shape,z)
    S=jax.ShapeDtypeStruct
    return pl.pallas_call(kernel,
        grid_spec=pltpu.PrefetchScalarGridSpec(num_scalar_prefetch=1,grid=(9,),
            in_specs=[pl.BlockSpec((ROWS,G),ia)]*2+[pl.BlockSpec((ROWS,G),ib)]*2+[full(qp),full(dp_),full(k),full(v),full(ka),full(va),full(kb),full(vb)],
            out_specs=[pl.BlockSpec((ROWS,G),ia)]*2+[pl.BlockSpec((ROWS,G),ib)]*2+[pl.BlockSpec((ROWS,G),z)]*2+[pl.BlockSpec((2*LEN,2*HD),z),pl.BlockSpec((SLOTS,2*HD),z),pl.BlockSpec((SLOTS,2*HD),z)],
            scratch_shapes=[pltpu.VMEM((HD,2*LEN),jnp.float32)]*2+[pltpu.VMEM((HD,SLOTS),jnp.float32)]*2),
        out_shape=[S((SLOTS,2*G),bf),S((SLOTS,2*G),bf),S((SLOTS,G),bf),S((SLOTS,G),bf),S((ROWS,G),bf),S((ROWS,G),bf),S((2*LEN,2*HD),bf),S((SLOTS,2*HD),bf),S((SLOTS,2*HD),bf)],
        compiler_params=pltpu.CompilerParams(vmem_limit_bytes=56*1024*1024),
        name="attn")(info,qa,da,qb,db,qp,dp_,k,v,ka,va,kb,vb)


ALL=("x","z","core","head")
PAIR=("core","head")

def exchange(v,axes): return lax.all_to_all(v,axes,split_axis=0,concat_axis=0,tiled=True)
def swap(v): return lax.ppermute(v,"core",[(0,1),(1,0)])
def by_head(v,width):
    return v.reshape(8,4,2,width).transpose(2,1,0,3).reshape(8,8,width)
def to_rows(v,width):
    return v.reshape(2,4,8,width).transpose(2,1,0,3).reshape(8,8*width)

def shards(pq,pk,pv,pd,rq,rk,rv,rd,parent,lengths):
    x=lax.axis_index("x"); z=lax.axis_index("z"); core=lax.axis_index("core")
    G=GROUP*HD
    kv=jnp.concatenate([by_head(pk,HD),by_head(pv,HD)],axis=2)
    kv=jnp.broadcast_to(kv[None],(32,8,8,2*HD)).reshape(256,8,2*HD)
    kv=exchange(kv,ALL).reshape(32,8,8,2*HD)
    kv=kv.reshape(2*LEN,2*HD)
    qd=exchange(jnp.concatenate([by_head(pq,G),by_head(pd,G)],axis=2),PAIR).reshape(ROWS,2*G)
    other=1-core
    far=lambda v,w: swap(lax.dynamic_slice_in_dim(v,other*w,w,1))
    near=lambda v,w: lax.dynamic_slice_in_dim(v,core*w,w,1)
    qb,db,kb,vb=far(rq,G),far(rd,G),far(rk,HD),far(rv,HD)
    ka,va=near(rk,HD),near(rv,HD)
    mine=jnp.concatenate([parent,lengths])
    theirs=swap(mine)
    row=(x*8+z)*ROWS
    prompt=row//LEN
    info=jnp.stack([mine[0],theirs[0],mine[1],theirs[1],core,prompt,row-prompt*LEN,core]).astype(jnp.int32)
    oa,ga,ob,gb,op,gp,kvg,owna,ownb=call(info,rq,rd,qb,db,qd[:,:G],qd[:,G:],kv[:,:HD],kv[:,HD:],ka,va,kb,vb)
    ob,gb,ownb=swap(ob),swap(gb),swap(ownb)
    ro=lax.dynamic_update_slice_in_dim(oa,ob,other*G,1)
    rg=lax.dynamic_update_slice_in_dim(ga,gb,other*G,1)
    first=jnp.where(core==0,owna,ownb); second=jnp.where(core==0,ownb,owna)
    rkg=jnp.concatenate([first[:,:HD],second[:,:HD]],axis=1)
    rvg=jnp.concatenate([first[:,HD:],second[:,HD:]],axis=1)
    tot=exchange(kvg.reshape(256,8,2*HD),ALL).reshape(32,8,8,2*HD).astype(jnp.float32).sum(0).astype(jnp.bfloat16)
    back=exchange(jnp.concatenate([op.reshape(8,8,G),gp.reshape(8,8,G)],axis=2),PAIR)
    return (to_rows(back[:,:,:G],G),to_rows(back[:,:,G:],G),to_rows(tot[:,:,:HD],HD),to_rows(tot[:,:,HD:],HD),ro,rg,rkg,rvg)

def solution(mesh):
    fine=Mesh(mesh.devices.reshape(4,8,2,4),ALL)
    ctx=("x","z","core")
    rows=P(ALL,None); cols=P(ctx,"head")
    return jax.shard_map(shards,mesh=fine,in_specs=(rows,)*4+(cols,)*4+(P(ctx),)*2,out_specs=(rows,)*4+(cols,)*4,check_vma=False)
```

time: 546 us -> 148 us (0.27); the launches traced: 539 us -> 147 us
  waiting for transfers between devices: 357 us -> 53.3 us
  matrix products: 67 us -> 0 us
  Pallas kernels: 0 us -> 28.3 us
  other arithmetic: 26.2 us -> 3.31 us
  local copies, waits for them, and re-layouts: 31.4 us -> 14.6 us
  between operations: 15.9 us -> 2.24 us
  starting transfers between devices: 24.3 us -> 35.1 us
  blocking collectives: 17.5 us -> 9.73 us
    reduce_scatter x2 -> x0, waiting for transfers between devices: 224 us -> none  [the longest x1 138 us: shards(): lax.psum_scatter(jnp.concatenate(key_pieces, axis=0), 'ctx', scatter_dime...]
    all_gather x2 -> x0, waiting for transfers between devices: 128 us -> none  [the longest x1 76.9 us: shards(): lax.all_gather(own_value, 'ctx', axis=0, tiled=True)]
    dot_general x36 -> x0, matrix products: 67 us -> none  [the longest x6 14.8 us: forward_blocks(): jnp.einsum('nrk,kd->rnd', weights_half, value_head, preferred_element_typ...]
    all_to_all x6 -> x3, waiting for transfers between devices: 4.8 us -> 52.8 us  [exchange(): return lax.all_to_all(v, axes, split_axis=0, concat_axis=0, tiled=True)]
    pallas_call x0 -> x1, Pallas kernels: none -> 28.3 us  [call(): pl.pallas_call(kernel, grid_spec=pltpu.PrefetchScalarGridSpec(num_scalar_...]
    unnamed x125 -> x32, local copies, waits for them, and re-layouts: 28.5 us -> 1.72 us
    reduce_sum x6 -> x1, other arithmetic: 8.54 us -> 0.16 us  [shards(): exchange(kvg.reshape(256, 8, 2 * HD), ALL).reshape(32, 8, 8, 2 * HD)]
    all_to_all x2 -> x1, blocking collectives: 17.5 us -> 9.73 us  [exchange(): return lax.all_to_all(v, axes, split_axis=0, concat_axis=0, tiled=True)]
  transfers between devices with their start and end apart: 10 -> 11, of which waited for: 5 -> 4; matrix products, arithmetic and copies ran while one was open for 9% -> 8% of each run, Pallas kernels for 0% -> 0%
where the time goes in v1:
time: 148 us; the launch traced here: 147 us
  waiting for transfers between devices  53.3 us (36%)
  starting transfers between devices  35.1 us (24%)
  Pallas kernels  28.3 us (19%)
  local copies, waits for them, and re-layouts  14.6 us (10%)
  blocking collectives  9.73 us (7%)
  other arithmetic  3.31 us (2%)
  between operations  2.24 us (2%)
    all_to_all x3, waiting for transfers between devices, exchange(): return lax.all_to_all(v, axes, split_axis=0, concat_axis=0, tiled=True)  52.8 us
    all_to_all x3, starting transfers between devices, exchange(): return lax.all_to_all(v, axes, split_axis=0, concat_axis=0, tiled=True)  29.2 us
    pallas_call x1, Pallas kernels, call(): pl.pallas_call(kernel, grid_spec=pltpu.PrefetchScalarGridSpec(num_scalar_...  28.3 us
    all_to_all x1, blocking collectives, exchange(): return lax.all_to_all(v, axes, split_axis=0, concat_axis=0, tiled=True)  9.73 us
    ppermute x8, starting transfers between devices, swap(): return lax.ppermute(v, 'core', [(0, 1), (1, 0)])  5.93 us
    dynamic_slice x4, local copies, waits for them, and re-layouts, shards(): far = lambda v, w: swap(lax.dynamic_slice_in_dim(v, other * w, w, 1))  3.86 us
  transfers between devices with their start and end apart: 11, of which 4 were waited for; matrix products, arithmetic and copies ran while one was open for 8% of the time, Pallas kernels for 0%

profile of v1, /device:TPU:1, one launch (start us, length us, event | category | flops | bytes accessed | tf_op | source)
XLA Modules:
  0.0 146.6 jit_solution(10483670165590978275)
XLA Ops:
  0.6 0.9 copy.26
  1.6 0.7 pad_maximum_fusion
  2.3 6.7 %all-to-all-start = ((bf16[8,8,2048]{2,1,0:T(8,128)(2,1)}), bf16[8,8,2048]{2,1,0:T(8,128)(2,1)S(1)}, u32[]{:S(2)}, u32[]{:S(2)}) async-start(bf16[8,8,2048]{2,1,0:T(8,128)(2,1)} %pad_maximum_fusion), calls=%async_computation | async-start | bytes 524288 | tf_op jit(solution)/shard_map/all_to_all | solution.py:120
  9.1 0.7 copy-done.10
  9.8 5.8 %all-to-all-done = bf16[8,8,2048]{2,1,0:T(8,128)(2,1)S(1)} async-done(((bf16[8,8,2048]{2,1,0:T(8,128)(2,1)}), bf16[8,8,2048]{2,1,0:T(8,128)(2,1)S(1)}, u32[]{:S(2)}, u32[]{:S(2)}) %all-to-all-start) | async-done | bytes 262176 | tf_op jit(solution)/shard_map/all_to_all | solution.py:120
  15.6 1.1 broadcast_in_dim.2
  16.7 12.5 %all-to-all-start.1 = ((bf16[256,8,256]{2,1,0:T(8,128)(2,1)}), bf16[256,8,256]{2,1,0:T(8,128)(2,1)S(1)}, u32[]{:S(2)}, u32[]{:S(2)}) async-start(bf16[256,8,256]{2,1,0:T(8,128)(2,1)} %bitcast.16), calls=%async_computation.1 | async-start | bytes 2097152 | tf_op jit(solution)/shard_map/all_to_all | solution.py:120
  30.7 2.2 %collective-permute-start = (s32[2]{0:T(128)S(1)}, s32[2]{0:T(128)S(1)}, u32[]{:S(2)}, u32[]{:S(2)}) collective-permute-start(s32[2]{0:T(128)S(1)} %pad_add_fusion), channel_id=1, source_target_pairs={{0,4},{4,0},{1,5},{5,1},{2,6},{6,2},{3,7},{7,3},{8,12},{12,8},{9,1... | collective-permute-start | bytes 32 | tf_op jit(solution)/shard_map/ppermute | solution.py:121
  32.9 0.7 constant_dynamic-slice_fusion.1
  33.6 1.5 %constant_dynamic-slice_fusion = (bf16[256,128]{1,0:T(8,128)(2,1)}, bf16[256,128]{1,0:T(8,128)(2,1)}) fusion(bf16[256,256]{1,0:T(8,128)(2,1)} %param.16, s32[]{:T(128)S(6)} %select_n.34, s32[]{:T(128)S(6)} %select_n.33), kind=kLoop, calls=%fused_computation.9 | loop fusion | bytes 262152 | tf_op jit(solution)/shard_map/dynamic_slice | solution.py:136
  35.1 0.5 collective-permute-start.4
  35.6 0.8 constant_dynamic-slice_fusion.4
  36.4 0.8 constant_dynamic-slice_fusion.5
  37.3 0.5 collective-permute-start.1
  37.8 0.6 fusion.6
  38.3 1.9 %stack.16.info = s32[8]{0:T(128)} concatenate(s32[1]{0:T(128)S(6)} %copy.36, s32[1]{0:T(128)} %get-tuple-element.45, s32[1]{0:T(128)S(6)} %copy.37, s32[1]{0:T(128)} %get-tuple-element.44, s32[1]{0:T(128)} %bitcast, s32[1]{0:T(128)} %bitcast.1, s32[1]{0:T(128)} %bitcast.2, s32[1]{0:T(128)} %bitcast), dimensions={0} | concatenate | bytes 64 | tf_op jit(solution)/shard_map/stack | solution.py:144
  40.2 0.7 fusion.2
  40.9 20.7 %all-to-all-done.1 = bf16[256,8,256]{2,1,0:T(8,128)(2,1)S(1)} async-done(((bf16[256,8,256]{2,1,0:T(8,128)(2,1)}), bf16[256,8,256]{2,1,0:T(8,128)(2,1)S(1)}, u32[]{:S(2)}, u32[]{:S(2)}) %all-to-all-start.1) | async-done | bytes 1048608 | tf_op jit(solution)/shard_map/all_to_all | solution.py:120
  61.7 1.1 fusion
  62.8 0.6 copy-done.7
  63.7 28.3 %attn.1 = (bf16[256,2048]{1,0:T(8,128)(2,1)}, bf16[256,2048]{1,0:T(8,128)(2,1)}, bf16[256,1024]{1,0:T(8,128)(2,1)}, bf16[256,1024]{1,0:T(8,128)(2,1)}, bf16[64,1...) custom-call(s32[8]{0:T(128)} %stack.16.info, ...), custom_call_target="tpu_custom_call" | custom-call | tf_op jit(solution)/shard_map/attn/pallas_call | solution.py:107
  92.1 1.0 pad_maximum_fusion.1
  93.1 9.7 %all_to_all.20 = bf16[8,8,2048]{2,1,0:T(8,128)(2,1)S(1)} all-to-all(bf16[8,8,2048]{2,1,0:T(8,128)(2,1)S(1)} %pad_maximum_fusion.1), channel_id=1, replica_groups=mesh['x'=4,'z'=8,'core'=2,'head'=4] {'core','head'}, dimensions={0} | all-to-all | bytes 524288 | tf_op jit(solution)/shard_map/all_to_all | solution.py:120
  102.8 10.0 %all-to-all-start.3 = ((bf16[256,8,256]{2,1,0:T(8,128)(2,1)}), bf16[256,8,256]{2,1,0:T(8,128)(2,1)S(1)}, u32[]{:S(2)}, u32[]{:S(2)}) async-start(bf16[256,8,256]{2,1,0:T(8,128)(2,1)} %bitcast.26), calls=%async_computation.3 | async-start | bytes 2097152 | tf_op jit(solution)/shard_map/all_to_all | solution.py:120
  112.8 2.2 %collective-permute-start.7 = (bf16[256,256]{1,0:T(8,128)(2,1)S(1)}, bf16[256,256]{1,0:T(8,128)(2,1)S(1)}, u32[]{:S(2)}, u32[]{:S(2)}) collective-permute-start(bf16[256,256]{1,0:T(8,128)(2,1)S(1)} %copy-done.15), channel_id=1, source_target_pairs={{0,4},{4,0},{1,5},{5,1},{2,6},{6,2},{3,7},{7,3},{8,12},{12,8},{9,1... | collective-permute-start | bytes 393224 | tf_op jit(solution)/shard_map/ppermute | solution.py:121
  116.1 0.7 pad_maximum_fusion.3
  116.8 0.7 pad_maximum_fusion.2
  117.5 0.7 copy.31
  118.2 0.7 copy.30
  119.0 26.3 %all-to-all-done.3 = bf16[256,8,256]{2,1,0:T(8,128)(2,1)S(1)} async-done(((bf16[256,8,256]{2,1,0:T(8,128)(2,1)}), bf16[256,8,256]{2,1,0:T(8,128)(2,1)S(1)}, u32[]{:S(2)}, u32[]{:S(2)}) %all-to-all-start.3) | async-done | bytes 1048608 | tf_op jit(solution)/shard_map/all_to_all | solution.py:120
  145.4 0.6 copy.33
  146.0 0.6 copy.32
  (54 shorter events, 2.0 us)
Async XLA Ops:
  0.6 1.0 copy-start.5
  2.3 6.7 %copy-start.9 = (bf16[8,1024]{1,0:T(8,128)(2,1)S(1)}, bf16[8,1024]{1,0:T(8,128)(2,1)}, u32[]{:S(2)}) copy-start(bf16[8,1024]{1,0:T(8,128)(2,1)} %param.11) | copy-start | bytes 49156
  2.3 13.3 %all-to-all-start = ((bf16[8,8,2048]{2,1,0:T(8,128)(2,1)}), bf16[8,8,2048]{2,1,0:T(8,128)(2,1)S(1)}, u32[]{:S(2)}, u32[]{:S(2)}) async-start(bf16[8,8,2048]{2,1,0:T(8,128)(2,1)} %pad_maximum_fusion), calls=%async_computation | async-start | bytes 524288 | tf_op jit(solution)/shard_map/all_to_all | solution.py:120
  9.1 0.7 copy-start.10
  16.7 16.2 %copy-start.6 = (bf16[256,256]{1,0:T(8,128)(2,1)S(1)}, bf16[256,256]{1,0:T(8,128)(2,1)}, u32[]{:S(2)}) copy-start(bf16[256,256]{1,0:T(8,128)(2,1)} %param.15) | copy-start | bytes 393220
  16.7 18.9 %copy-start.1 = (bf16[256,2048]{1,0:T(8,128)(2,1)S(1)}, bf16[256,2048]{1,0:T(8,128)(2,1)}, u32[]{:S(2)}) copy-start(bf16[256,2048]{1,0:T(8,128)(2,1)} %da.1) | copy-start | bytes 3145732
  16.7 45.0 %all-to-all-start.1 = ((bf16[256,8,256]{2,1,0:T(8,128)(2,1)}), bf16[256,8,256]{2,1,0:T(8,128)(2,1)S(1)}, u32[]{:S(2)}, u32[]{:S(2)}) async-start(bf16[256,8,256]{2,1,0:T(8,128)(2,1)} %bitcast.16), calls=%async_computation.1 | async-start | bytes 2097152 | tf_op jit(solution)/shard_map/all_to_all | solution.py:120
  29.2 7.2 %copy-start = (bf16[256,2048]{1,0:T(8,128)(2,1)S(1)}, bf16[256,2048]{1,0:T(8,128)(2,1)}, u32[]{:S(2)}) copy-start(bf16[256,2048]{1,0:T(8,128)(2,1)} %qa.1) | copy-start | bytes 3145732
  30.7 7.1 %collective-permute-start = (s32[2]{0:T(128)S(1)}, s32[2]{0:T(128)S(1)}, u32[]{:S(2)}, u32[]{:S(2)}) collective-permute-start(s32[2]{0:T(128)S(1)} %pad_add_fusion), channel_id=1, source_target_pairs={{0,4},{4,0},{1,5},{5,1},{2,6},{6,2},{3,7},{7,3},{8,12},{12,8},{9,1... | collective-permute-start | bytes 32 | tf_op jit(solution)/shard_map/ppermute | solution.py:121
  33.5 29.2 %collective-permute-start.3 = (bf16[256,128]{1,0:T(8,128)(2,1)}, bf16[256,128]{1,0:T(8,128)(2,1)S(1)}, u32[]{:S(2)}, u32[]{:S(2)}) collective-permute-start(bf16[256,128]{1,0:T(8,128)(2,1)} %get-tuple-element.40), channel_id=1, source_target_pairs={{0,4},{4,0},{1,5},{5,1},{2,6},{6,2},{3,7},{7,3},{8,12},{12,8},{9,1... | collective-permute-start | bytes 196616 | tf_op jit(solution)/shard_map/ppermute | solution.py:121
  35.1 27.7 %collective-permute-start.4 = (bf16[256,128]{1,0:T(8,128)(2,1)}, bf16[256,128]{1,0:T(8,128)(2,1)S(1)}, u32[]{:S(2)}, u32[]{:S(2)}) collective-permute-start(bf16[256,128]{1,0:T(8,128)(2,1)} %get-tuple-element.38), channel_id=1, source_target_pairs={{0,4},{4,0},{1,5},{5,1},{2,6},{6,2},{3,7},{7,3},{8,12},{12,8},{9,1... | collective-permute-start | bytes 196616 | tf_op jit(solution)/shard_map/ppermute | solution.py:121
  36.4 26.4 %collective-permute-start.2 = (bf16[256,1024]{1,0:T(8,128)(2,1)}, bf16[256,1024]{1,0:T(8,128)(2,1)S(1)}, u32[]{:S(2)}, u32[]{:S(2)}) collective-permute-start(bf16[256,1024]{1,0:T(8,128)(2,1)} %constant_dynamic-slice_fusion.4), channel_id=1, source_target_pairs={{0,4},{4,0},{1,5},{5,1},{2,6},{6,2},{3,7},{7,3},{8,12},{12,8},{9,1... | collective-permute-start | bytes 1572872 | tf_op jit(solution)/shard_map/ppermute | solution.py:121
  37.3 25.5 %collective-permute-start.1 = (bf16[256,1024]{1,0:T(8,128)(2,1)}, bf16[256,1024]{1,0:T(8,128)(2,1)S(1)}, u32[]{:S(2)}, u32[]{:S(2)}) collective-permute-start(bf16[256,1024]{1,0:T(8,128)(2,1)} %constant_dynamic-slice_fusion.5), channel_id=1, source_target_pairs={{0,4},{4,0},{1,5},{5,1},{2,6},{6,2},{3,7},{7,3},{8,12},{12,8},{9,1... | collective-permute-start | bytes 1572872 | tf_op jit(solution)/shard_map/ppermute | solution.py:121
  62.7 0.6 copy-start.7
  62.7 0.6 copy-start.8
  62.8 0.8 copy-start.2
  62.8 1.0 copy-start.3
  102.8 10.0 %copy-start.15 = (bf16[256,256]{1,0:T(8,128)(2,1)S(1)}, bf16[256,256]{1,0:T(8,128)(2,1)}, u32[]{:S(2)}) copy-start(bf16[256,256]{1,0:T(8,128)(2,1)} %get-tuple-element.25) | copy-start | bytes 393220
  102.8 13.2 %copy-start.4 = (bf16[256,256]{1,0:T(8,128)(2,1)S(1)}, bf16[256,256]{1,0:T(8,128)(2,1)}, u32[]{:S(2)}) copy-start(bf16[256,256]{1,0:T(8,128)(2,1)} %get-tuple-element.24) | copy-start | bytes 393220
  102.8 42.5 %all-to-all-start.3 = ((bf16[256,8,256]{2,1,0:T(8,128)(2,1)}), bf16[256,8,256]{2,1,0:T(8,128)(2,1)S(1)}, u32[]{:S(2)}, u32[]{:S(2)}) async-start(bf16[256,8,256]{2,1,0:T(8,128)(2,1)} %bitcast.26), calls=%async_computation.3 | async-start | bytes 2097152 | tf_op jit(solution)/shard_map/all_to_all | solution.py:120
  112.8 3.2 %collective-permute-start.7 = (bf16[256,256]{1,0:T(8,128)(2,1)S(1)}, bf16[256,256]{1,0:T(8,128)(2,1)S(1)}, u32[]{:S(2)}, u32[]{:S(2)}) collective-permute-start(bf16[256,256]{1,0:T(8,128)(2,1)S(1)} %copy-done.15), channel_id=1, source_target_pairs={{0,4},{4,0},{1,5},{5,1},{2,6},{6,2},{3,7},{7,3},{8,12},{12,8},{9,1... | collective-permute-start | bytes 393224 | tf_op jit(solution)/shard_map/ppermute | solution.py:121
  115.0 3.8 %collective-permute-start.5 = (bf16[256,1024]{1,0:T(8,128)(2,1)}, bf16[256,1024]{1,0:T(8,128)(2,1)S(1)}, u32[]{:S(2)}, u32[]{:S(2)}) collective-permute-start(bf16[256,1024]{1,0:T(8,128)(2,1)} %get-tuple-element.21), channel_id=1, source_target_pairs={{0,4},{4,0},{1,5},{5,1},{2,6},{6,2},{3,7},{7,3},{8,12},{12,8},{9,1... | collective-permute-start | bytes 1572872 | tf_op jit(solution)/shard_map/ppermute | solution.py:121
  115.1 3.7 %collective-permute-start.6 = (bf16[256,1024]{1,0:T(8,128)(2,1)}, bf16[256,1024]{1,0:T(8,128)(2,1)S(1)}, u32[]{:S(2)}, u32[]{:S(2)}) collective-permute-start(bf16[256,1024]{1,0:T(8,128)(2,1)} %get-tuple-element.23), channel_id=1, source_target_pairs={{0,4},{4,0},{1,5},{5,1},{2,6},{6,2},{3,7},{7,3},{8,12},{12,8},{9,1... | collective-permute-start | bytes 1572872 | tf_op jit(solution)/shard_map/ppermute | solution.py:121
  116.1 2.8 %copy-start.13 = (bf16[256,2048]{1,0:T(8,128)(2,1)S(1)}, bf16[256,2048]{1,0:T(8,128)(2,1)}, u32[]{:S(2)}) copy-start(bf16[256,2048]{1,0:T(8,128)(2,1)} %get-tuple-element.20) | copy-start | bytes 3145732
  117.5 1.4 copy-start.11
  118.9 26.5 %copy-start.14 = (bf16[256,2048]{1,0:T(8,128)(2,1)}, bf16[256,2048]{1,0:T(8,128)(2,1)S(1)}, u32[]{:S(2)}) copy-start(bf16[256,2048]{1,0:T(8,128)(2,1)S(1)} %constant_dynamic-update-slice_fusion.1) | copy-start | bytes 3145732
  119.0 27.7 %copy-start.12 = (bf16[256,2048]{1,0:T(8,128)(2,1)}, bf16[256,2048]{1,0:T(8,128)(2,1)S(1)}, u32[]{:S(2)}) copy-start(bf16[256,2048]{1,0:T(8,128)(2,1)S(1)} %constant_dynamic-update-slice_fusion) | copy-start | bytes 3145732

commit v2 on v1

v2 whole, which is shorter than its diff:
```python
import functools
import math

import jax
import jax.numpy as jnp
from jax import lax
from jax.experimental import pallas as pl
from jax.experimental.pallas import tpu as pltpu
from jax.sharding import Mesh, PartitionSpec as P
HD=128; GROUP=8; LEN=1024; SLOTS=256; ROWS=64; M=ROWS*GROUP; SLAB=512
SCALE=1.0/math.sqrt(HD); LOG2E=math.log2(math.e)
NT=(((1,),(1,)),((),())); NN=(((1,),(0,)),((),()))
def dot(a,b,dims=NN): return lax.dot_general(a,b,dims,preferred_element_type=jnp.float32)
def stack(x): return jnp.concatenate([x[:,h*HD:(h+1)*HD] for h in range(GROUP)],axis=0)
def unstack(x): return jnp.concatenate([x[h*ROWS:(h+1)*ROWS] for h in range(GROUP)],axis=1)
F=jnp.float32; H=jnp.bfloat16
def tr(x): return x.astype(F).T.astype(H)

class Block: pass

def scores(t):
    t.s=[dot(t.q,key,NT) if vis is None else jnp.where(vis,dot(t.q,key,NT),-1e30) for key,val,vis in t.parts]

def softmax(t):
    m=functools.reduce(jnp.maximum,[jnp.max(s,axis=1,keepdims=True) for s in t.s])
    c=SCALE*LOG2E
    mc=m*c
    t.w=[jnp.exp2(s*c-mc) for s in t.s]
    t.wh=[x.astype(H) for x in t.w]

def output(t):
    oe=functools.reduce(jnp.add,[dot(x,part[1]) for x,part in zip(t.wh,t.parts)])
    inv=1.0/oe[:,HD:]
    if t.live is not None: inv=inv*t.live
    t.o=(oe[:,:HD]*inv).astype(H)
    dos=t.do.astype(F)*inv
    rd=jnp.sum(t.o.astype(F)*dos,axis=1,keepdims=True)
    hi=(-rd).astype(H).astype(F)
    lo=-rd-hi
    lane=lax.broadcasted_iota(jnp.int32,(t.q.shape[0],HD),1)
    ext=jnp.where(lane==0,hi,jnp.where(lane==1,lo,0.0)).astype(H)
    t.dE=jnp.concatenate([dos.astype(H),ext],axis=1)
    t.dT=dos.T.astype(H)
    t.qT=tr(t.q)

def score_grad(t):
    t.ds=[(x*dot(t.dE,part[1],NT)).astype(H) for x,part in zip(t.w,t.parts)]

def query_grad(t):
    t.dq=(functools.reduce(jnp.add,[dot(x,part[0]) for x,part in zip(t.ds,t.parts)])*SCALE).astype(H)

def pieces(q,do,parts,live):
    halves=[]
    for i in range(2):
        cut=lambda v: None if v is None else v[i*M//2:(i+1)*M//2]
        t=Block(); t.q=cut(q); t.do=cut(do); t.live=cut(live)
        t.parts=[(key,val,cut(vis)) for key,val,vis in parts]
        halves.append(t)
    for step in (scores,softmax,output,score_grad,query_grad):
        for t in halves: step(t)
    a,b=halves
    dvs=[dot(a.dT,x)+dot(b.dT,y) for x,y in zip(a.wh,b.wh)]
    dks=[dot(a.qT,x)+dot(b.qT,y) for x,y in zip(a.ds,b.ds)]
    return jnp.concatenate([a.o,b.o]),jnp.concatenate([a.dq,b.dq]),list(zip(dks,dvs))

HALF=SLAB//2
def slab_at(x,d): return pl.multiple_of(lax.rem(x+d,4)*SLAB,SLAB)

def kernel(info,qa,da,qb,db,qd,s0,s1,s2,s3,ka,va,kb,vb,
           oa,ga,ob,gb,og,g0,g1,g2,g3,g4,owna,ownb, kg,vg,okg,ovg,ks,vs):
    u=pl.program_id(0); x=info[7]
    @pl.when(u==0)
    def _():
        kg[...]=jnp.zeros_like(kg); vg[...]=jnp.zeros_like(vg)
        vs[:,HD:]=jnp.ones((2*LEN,HD),H)
        for ref,d,first in ((s0,0,0),(s1,3,0),(s2,1,0),(s3,2,0)):
            n=ref.shape[0]; at=slab_at(x,d)+first
            ks[pl.ds(at,n),:]=ref[:,:HD]
            vs[pl.ds(at,n),:HD]=ref[:,HD:]
    r=u//4; b=u%4
    def add(off,g):
        kg[:,pl.ds(off,LEN)]+=g[0]; vg[:,pl.ds(off,LEN)]+=g[1]
    def prompt(source):
        off=pl.multiple_of(source*LEN,LEN)
        return off,(ks[pl.ds(off,LEN),:],vs[pl.ds(off,LEN),:])
    def reply(slot,q_ref,d_ref,ko,vo,o_ref,g_ref,own_ref):
        length=info[2+slot]; source=info[slot]
        @pl.when(b==0)
        def _():
            okg[...]=jnp.zeros_like(okg); ovg[...]=jnp.zeros_like(ovg)
        alive=b*ROWS<length
        @pl.when(jnp.logical_not(alive))
        def _():
            o_ref[...]=jnp.zeros_like(o_ref); g_ref[...]=jnp.zeros_like(g_ref)
        @pl.when(alive)
        def _():
            off,main=prompt(source)
            row=b*ROWS+lax.broadcasted_iota(jnp.int32,(M,1),0)%ROWS
            vis=row>=lax.broadcasted_iota(jnp.int32,(M,SLOTS),1)
            live=(row<length).astype(F)
            o,dq,g=pieces(stack(q_ref[...]),stack(d_ref[...]),[main+(None,),(ko[...],jnp.concatenate([vo[...],jnp.ones((SLOTS,HD),H)],axis=1),vis)],live)
            o_ref[...]=unstack(o); g_ref[...]=unstack(dq)
            add(off,g[0])
            okg[...]+=g[1][0]; ovg[...]+=g[1][1]
        @pl.when(b==3)
        def _():
            own_ref[:,:HD]=(okg[...]*SCALE).T.astype(H)
            own_ref[:,HD:]=ovg[...].T.astype(H)
    @pl.when(r==0)
    def _(): reply(0,qa,da,ka,va,oa,ga,owna)
    @pl.when(r==1)
    def _(): reply(1,qb,db,kb,vb,ob,gb,ownb)
    @pl.when(u==8)
    def _():
        off,main=prompt(info[5])
        row=info[6]+lax.broadcasted_iota(jnp.int32,(M,1),0)%ROWS
        vis=row>=lax.broadcasted_iota(jnp.int32,(M,LEN),1)
        o,dq,g=pieces(stack(qd[:,:G]),stack(qd[:,G:]),[main+(vis,)],None)
        og[:,:G]=unstack(o); og[:,G:]=unstack(dq)
        add(off,g[0])
        for ref,d,first in ((g0,0,0),(g1,1,0),(g2,3,0),(g3,2,0),(g4,2,HALF)):
            n=ref.shape[0]; at=slab_at(x,d)+first
            ref[:,:HD]=(kg[:,pl.ds(at,n)]*SCALE).T.astype(H)
            ref[:,HD:]=vg[:,pl.ds(at,n)].T.astype(H)

G=GROUP*HD
def call(info,qa,da,qb,db,qd,slabs,ka,va,kb,vb):
    near=pl.BlockSpec((ROWS,G),lambda u,s:(jnp.minimum(u,3),s[4]))
    far=pl.BlockSpec((ROWS,G),lambda u,s:(jnp.clip(u-4,0,3),0))
    full=lambda *shape: pl.BlockSpec(shape,lambda u,s:(0,0))
    half=pl.BlockSpec((SLOTS,HD),lambda u,s:(0,s[4]))
    out=lambda *shape: jax.ShapeDtypeStruct(shape,H)
    whole=full(SLAB,2*HD); part=full(HALF,2*HD); own=full(SLOTS,2*HD)
    scratch=[(HD,2*LEN,F),(HD,2*LEN,F),(HD,SLOTS,F),(HD,SLOTS,F),(2*LEN,HD,H),(2*LEN,2*HD,H)]
    return pl.pallas_call(kernel,
        grid_spec=pltpu.PrefetchScalarGridSpec(num_scalar_prefetch=1,grid=(9,),
            in_specs=[near,near,far,far,full(ROWS,2*G)]+[whole]*4+[half,half]+[full(SLOTS,HD)]*2,
            out_specs=[near,near,far,far,full(ROWS,2*G)]+[whole]*3+[part]*2+[own]*2,
            scratch_shapes=[pltpu.VMEM(s[:2],s[2]) for s in scratch]),
        out_shape=[out(SLOTS,2*G),out(SLOTS,2*G),out(SLOTS,G),out(SLOTS,G),out(ROWS,2*G)]+[out(SLAB,2*HD)]*3+[out(HALF,2*HD)]*2+[out(SLOTS,2*HD)]*2,
        compiler_params=pltpu.CompilerParams(vmem_limit_bytes=56*1024*1024),
        name="attn")(info,qa,da,qb,db,qd,*slabs,ka,va,kb,vb)

ALL=("x","z","core","head")
PLANE=("z","core","head")
PAIR=("core","head")

def exchange(v,axes): return lax.all_to_all(v,axes,split_axis=0,concat_axis=0,tiled=True)
def swap(v): return lax.ppermute(v,"core",[(0,1),(1,0)])
def shift(v,d): return lax.ppermute(v,"x",[(i,(i+d)%4) for i in range(4)])
def by_head(v,width):
    return v.reshape(8,4,2,width).transpose(2,1,0,3).reshape(8,8,width)
def to_rows(v,width):
    return v.reshape(2,4,8,width).transpose(2,1,0,3).reshape(8,8*width)

def shards(pq,pk,pv,pd,rq,rk,rv,rd,parent,lengths):
    x=lax.axis_index("x"); z=lax.axis_index("z"); core=lax.axis_index("core")
    kv=jnp.concatenate([by_head(pk,HD),by_head(pv,HD)],axis=2)
    kv=jnp.broadcast_to(kv[None],(8,8,8,2*HD)).reshape(64,8,2*HD)
    slab=exchange(kv,PLANE).reshape(SLAB,2*HD)
    slabs=(slab,shift(slab,1),shift(slab,3),shift(slab,2))
    other=1-core
    far=lambda v,w: swap(lax.dynamic_slice_in_dim(v,other*w,w,1))
    kb,vb=far(rk,HD),far(rv,HD)
    qb,db=far(rq,G),far(rd,G)
    theirs=swap(jnp.concatenate([parent,lengths]))
    qd=exchange(jnp.concatenate([by_head(pq,G),by_head(pd,G)],axis=2),PAIR).reshape(ROWS,2*G)
    row=(x*8+z)*ROWS
    prompt=row//LEN
    at=lax.broadcasted_iota(jnp.int32,(8,),0)
    info=jnp.zeros((8,),jnp.int32)
    for i,v in enumerate((parent[0],theirs[0],lengths[0],theirs[1],core,prompt,row-prompt*LEN,x)):
        info=jnp.where(at==i,v,info)
    oa,ga,ob,gb,og,g0,g1,g2,g3,g4,owna,ownb=call(info,rq,rd,qb,db,qd,slabs,rk,rv,kb,vb)
    g4=shift(shift(g4,3),3)
    opposite=jnp.concatenate([shift(g3,2),g4],axis=0)
    part=(g0.astype(F)+shift(g1,1).astype(F)+shift(g2,3).astype(F)+opposite.astype(F)).astype(H)
    ownb=swap(ownb)
    og,ownb=lax.optimization_barrier((og,ownb))
    back=exchange(og.reshape(8,8,2*G),PAIR)
    back,part=lax.optimization_barrier((back,part))
    tot=exchange(part.reshape(64,8,2*HD),PLANE).reshape(8,8,8,2*HD).astype(F).sum(0).astype(H)
    ob,gb=swap(ob),swap(gb)
    ro=lax.dynamic_update_slice_in_dim(oa,ob,other*G,1)
    rg=lax.dynamic_update_slice_in_dim(ga,gb,other*G,1)
    first=jnp.where(core==0,owna,ownb); second=jnp.where(core==0,ownb,owna)
    rkg=jnp.concatenate([first[:,:HD],second[:,:HD]],axis=1)
    rvg=jnp.concatenate([first[:,HD:],second[:,HD:]],axis=1)
    return (to_rows(back[:,:,:G],G),to_rows(back[:,:,G:],G),to_rows(tot[:,:,:HD],HD),to_rows(tot[:,:,HD:],HD),ro,rg,rkg,rvg)

def solution(mesh):
    fine=Mesh(mesh.devices.reshape(4,8,2,4),ALL)
    ctx=("x","z","core")
    rows=P(ALL,None); cols=P(ctx,"head")
    return jax.shard_map(shards,mesh=fine,in_specs=(rows,)*4+(cols,)*4+(P(ctx),)*2,out_specs=(rows,)*4+(cols,)*4,check_vma=False)
```

time: 148 us -> 110 us (0.74)
  waiting for transfers between devices: 53.3 us -> 23.1 us
  starting transfers between devices: 35.1 us -> 45.2 us
  blocking collectives: 9.73 us -> 0 us
  Pallas kernels: 28.3 us -> 20.9 us
  local copies, waits for them, and re-layouts: 14.6 us -> 11.8 us
  other arithmetic: 3.31 us -> 4.87 us
    all_to_all x3 -> x4, waiting for transfers between devices: 52.8 us -> 19.2 us  [exchange(): return lax.all_to_all(v, axes, split_axis=0, concat_axis=0, tiled=True)]
    ppermute x0 -> x8, starting transfers between devices: none -> 13.3 us  [shift(): return lax.ppermute(v, 'x', [(i, (i + d) % 4) for i in range(4)])]
    all_to_all x1 -> x0, blocking collectives: 9.73 us -> none  [exchange(): return lax.all_to_all(v, axes, split_axis=0, concat_axis=0, tiled=True)]
    pallas_call x1, Pallas kernels: 28.3 us -> 20.9 us  [call(): pl.pallas_call(kernel, grid_spec=pltpu.PrefetchScalarGridSpec(num_scalar_...]
    ppermute x0 -> x8, waiting for transfers between devices: none -> 3.81 us  [shift(): return lax.ppermute(v, 'x', [(i, (i + d) % 4) for i in range(4)])]
    ppermute x8, starting transfers between devices: 5.93 us -> 3.72 us  [swap(): return lax.ppermute(v, 'core', [(0, 1), (1, 0)])]
    another operation x1 -> x0, local copies, waits for them, and re-layouts: 1.89 us -> none  [shards(): jnp.stack([mine[0], theirs[0], mine[1], theirs[1], core, prompt, row - pr...]
    select_n x0 -> x1, other arithmetic: none -> 1.81 us  [shards(): info = jnp.where(at == i, v, info)]
  transfers between devices with their start and end apart: 11 -> 20, of which waited for: 4 -> 5; matrix products, arithmetic and copies ran while one was open for 8% -> 10% of each run, Pallas kernels for 0% -> 0%
where the time goes in v2:
time: 110 us; the launch traced here: 108 us
  starting transfers between devices  45.2 us (41%)
  waiting for transfers between devices  23.1 us (21%)
  Pallas kernels  20.9 us (19%)
  local copies, waits for them, and re-layouts  11.8 us (11%)
  other arithmetic  4.87 us (4%)
  between operations  2.21 us (2%)
    all_to_all x4, starting transfers between devices, exchange(): return lax.all_to_all(v, axes, split_axis=0, concat_axis=0, tiled=True)  28.2 us
    pallas_call x1, Pallas kernels, call(): pl.pallas_call(kernel, grid_spec=pltpu.PrefetchScalarGridSpec(num_scalar_...  20.9 us
    all_to_all x4, waiting for transfers between devices, exchange(): return lax.all_to_all(v, axes, split_axis=0, concat_axis=0, tiled=True)  19.2 us
    ppermute x8, starting transfers between devices, shift(): return lax.ppermute(v, 'x', [(i, (i + d) % 4) for i in range(4)])  13.3 us
    ppermute x8, waiting for transfers between devices, shift(): return lax.ppermute(v, 'x', [(i, (i + d) % 4) for i in range(4)])  3.81 us
    ppermute x8, starting transfers between devices, swap(): return lax.ppermute(v, 'core', [(0, 1), (1, 0)])  3.72 us
    dynamic_slice x4, local copies, waits for them, and re-layouts, shards(): far = lambda v, w: swap(lax.dynamic_slice_in_dim(v, other * w, w, 1))  3.03 us
    unnamed x36, local copies, waits for them, and re-layouts  2.38 us
  transfers between devices with their start and end apart: 20, of which 5 were waited for; matrix products, arithmetic and copies ran while one was open for 10% of the time, Pallas kernels for 0%

profile of v2, /device:TPU:1, one launch (start us, length us, event | category | flops | bytes accessed | tf_op | source)
XLA Modules:
  0.0 108.1 jit_solution(5879590551883327530)
XLA Ops:
  0.6 0.8 copy.28
  1.5 0.7 copy.29
  2.2 0.7 broadcast_in_dim.39
  2.9 13.2 %all-to-all-start.1 = ((bf16[64,8,256]{2,1,0:T(8,128)(2,1)}), bf16[64,8,256]{2,1,0:T(8,128)(2,1)S(1)}, u32[]{:S(2)}, u32[]{:S(2)}) async-start(bf16[64,8,256]{2,1,0:T(8,128)(2,1)} %bitcast.17), calls=%async_computation.1 | async-start | bytes 524288 | tf_op jit(solution)/shard_map/all_to_all | solution.py:148
  16.1 1.5 %constant_dynamic-slice_fusion = bf16[256,128]{1,0:T(8,128)(2,1)} fusion(bf16[256,256]{1,0:T(8,128)(2,1)} %va.1, s32[]{:T(128)S(6)} %select_n.62), kind=kLoop, calls=%fused_computation.17 | loop fusion | bytes 131076 | tf_op jit(solution)/shard_map/dynamic_slice | solution.py:163
  18.0 1.5 %constant_dynamic-slice_fusion.1 = bf16[256,128]{1,0:T(8,128)(2,1)} fusion(bf16[256,256]{1,0:T(8,128)(2,1)} %ka.1, s32[]{:T(128)S(6)} %select_n.62), kind=kLoop, calls=%fused_computation.18 | loop fusion | bytes 131076 | tf_op jit(solution)/shard_map/dynamic_slice | solution.py:163
  22.2 0.9 copy-done.12
  23.1 5.2 %all-to-all-done.1 = bf16[64,8,256]{2,1,0:T(8,128)(2,1)S(1)} async-done(((bf16[64,8,256]{2,1,0:T(8,128)(2,1)}), bf16[64,8,256]{2,1,0:T(8,128)(2,1)S(1)}, u32[]{:S(2)}, u32[]{:S(2)}) %all-to-all-start.1) | async-done | bytes 262176 | tf_op jit(solution)/shard_map/all_to_all | solution.py:148
  28.4 2.7 %collective-permute-start.5 = (bf16[512,256]{1,0:T(8,128)(2,1)S(1)}, bf16[512,256]{1,0:T(8,128)(2,1)S(1)}, u32[]{:S(2)}, u32[]{:S(2)}) collective-permute-start(bf16[512,256]{1,0:T(8,128)(2,1)S(1)} %bitcast.44), channel_id=1, source_target_pairs={{0,128},{64,192},{128,0},{192,64},{1,129},{65,193},{129,1},{193,65... | collective-permute-start | bytes 786440 | tf_op jit(solution)/shard_map/ppermute | solution.py:150
  31.1 0.9 collective-permute-start.4
  32.6 0.7 pad_maximum_fusion
  33.3 6.2 %all-to-all-start = ((bf16[8,8,2048]{2,1,0:T(8,128)(2,1)}), bf16[8,8,2048]{2,1,0:T(8,128)(2,1)S(1)}, u32[]{:S(2)}, u32[]{:S(2)}) async-start(bf16[8,8,2048]{2,1,0:T(8,128)(2,1)} %pad_maximum_fusion), calls=%async_computation | async-start | bytes 524288 | tf_op jit(solution)/shard_map/all_to_all | solution.py:148
  40.1 1.8 %compare_select_fusion.7.info = s32[8]{0:T(128)} fusion(s32[]{:T(128)} %bitcast.42, s32[]{:T(128)} %bitcast.2, s32[]{:T(128)} %bitcast.43, s32[]{:T(128)} %bitcast, s32[]{:T(128)S(6)} %axis_index.41, s32[]{:T(128)S(6)} %select_n.52, s32[]{:T(128)S(6)} %sub.11, s32[]{:T(128)S(6)} %axis_index.35), kind=kLoop, calls=%fused_computation.14 | loop fusion | flops 128 | bytes 64 | tf_op jit(solution)/shard_map/jit(_where)/select_n | solution.py:173
  41.9 4.2 %all-to-all-done = bf16[8,8,2048]{2,1,0:T(8,128)(2,1)S(1)} async-done(((bf16[8,8,2048]{2,1,0:T(8,128)(2,1)}), bf16[8,8,2048]{2,1,0:T(8,128)(2,1)S(1)}, u32[]{:S(2)}, u32[]{:S(2)}) %all-to-all-start) | async-done | bytes 262176 | tf_op jit(solution)/shard_map/all_to_all | solution.py:148
  46.2 0.6 copy-done.3
  47.4 20.9 %attn.1 = (bf16[256,2048]{1,0:T(8,128)(2,1)}, bf16[256,2048]{1,0:T(8,128)(2,1)}, bf16[256,1024]{1,0:T(8,128)(2,1)}, bf16[256,1024]{1,0:T(8,128)(2,1)}, bf16[64,2...) custom-call(s32[8]{0:T(128)} %compare_select_fusion.7.info, ...), custom_call_target="tpu_custom_call" | custom-call | tf_op jit(solution)/shard_map/attn/pallas_call | solution.py:135
  68.8 2.2 %collective-permute-start.11 = (bf16[256,256]{1,0:T(8,128)(2,1)}, bf16[256,256]{1,0:T(8,128)(2,1)S(1)}, u32[]{:S(2)}, u32[]{:S(2)}) collective-permute-start(bf16[256,256]{1,0:T(8,128)(2,1)} %get-tuple-element.30), channel_id=1, source_target_pairs={{0,128},{64,192},{128,0},{192,64},{1,129},{65,193},{129,1},{193,65... | collective-permute-start | bytes 393224 | tf_op jit(solution)/shard_map/ppermute | solution.py:150
  71.0 4.1 %collective-permute-start.12 = (bf16[256,256]{1,0:T(8,128)(2,1)}, bf16[256,256]{1,0:T(8,128)(2,1)S(1)}, u32[]{:S(2)}, u32[]{:S(2)}) collective-permute-start(bf16[256,256]{1,0:T(8,128)(2,1)} %get-tuple-element.31), channel_id=1, source_target_pairs={{0,192},{64,0},{128,64},{192,128},{1,193},{65,1},{129,65},{193,129... | collective-permute-start | bytes 393224 | tf_op jit(solution)/shard_map/ppermute | solution.py:150
  75.1 2.7 %collective-permute-start.10 = (bf16[512,256]{1,0:T(8,128)(2,1)}, bf16[512,256]{1,0:T(8,128)(2,1)S(1)}, u32[]{:S(2)}, u32[]{:S(2)}) collective-permute-start(bf16[512,256]{1,0:T(8,128)(2,1)} %get-tuple-element.29), channel_id=1, source_target_pairs={{0,192},{64,0},{128,64},{192,128},{1,193},{65,1},{129,65},{193,129... | collective-permute-start | bytes 786440 | tf_op jit(solution)/shard_map/ppermute | solution.py:150
  77.8 1.3 %collective-permute-start.14 = (bf16[256,1024]{1,0:T(8,128)(2,1)}, bf16[256,1024]{1,0:T(8,128)(2,1)S(1)}, u32[]{:S(2)}, u32[]{:S(2)}) collective-permute-start(bf16[256,1024]{1,0:T(8,128)(2,1)} %get-tuple-element.35), channel_id=1, source_target_pairs={{0,4},{4,0},{1,5},{5,1},{2,6},{6,2},{3,7},{7,3},{8,12},{12,8},{9,1... | collective-permute-start | bytes 1572872 | tf_op jit(solution)/shard_map/ppermute | solution.py:149
  79.1 3.5 %all-to-all-start.2 = ((bf16[8,8,2048]{2,1,0:T(8,128)(2,1)}), bf16[8,8,2048]{2,1,0:T(8,128)(2,1)S(1)}, u32[]{:S(2)}, u32[]{:S(2)}) async-start(bf16[8,8,2048]{2,1,0:T(8,128)(2,1)} %bitcast.54), calls=%async_computation.2 | async-start | bytes 524288 | tf_op jit(solution)/shard_map/all_to_all | solution.py:148
  82.8 0.7 pad_maximum_fusion.2
  84.0 3.8 %collective-permute-done.13 = bf16[256,256]{1,0:T(8,128)(2,1)S(1)} collective-permute-done((bf16[256,256]{1,0:T(8,128)(2,1)S(1)}, bf16[256,256]{1,0:T(8,128)(2,1)S(1)}, u32[]{:S(2)}, u32[]{:S(2)}) %collective-permute-start.13) | collective-permute-done | bytes 131104 | tf_op jit(solution)/shard_map/ppermute | solution.py:150
  87.8 0.8 add_convert_fusion
  89.1 5.3 %all-to-all-start.3 = ((bf16[64,8,256]{2,1,0:T(8,128)(2,1)}), bf16[64,8,256]{2,1,0:T(8,128)(2,1)S(1)}, u32[]{:S(2)}, u32[]{:S(2)}) async-start(bf16[64,8,256]{2,1,0:T(8,128)(2,1)} %bitcast.26), calls=%async_computation.3 | async-start | bytes 524288 | tf_op jit(solution)/shard_map/all_to_all | solution.py:148
  94.5 0.7 pad_maximum_fusion.1
  95.2 0.7 copy.31
  95.8 0.7 copy.30
  96.5 0.8 constant_dynamic-update-slice_fusion.1
  97.4 9.4 %all-to-all-done.3 = bf16[64,8,256]{2,1,0:T(8,128)(2,1)S(1)} async-done(((bf16[64,8,256]{2,1,0:T(8,128)(2,1)}), bf16[64,8,256]{2,1,0:T(8,128)(2,1)S(1)}, u32[]{:S(2)}, u32[]{:S(2)}) %all-to-all-start.3) | async-done | bytes 262176 | tf_op jit(solution)/shard_map/all_to_all | solution.py:148
  106.8 0.6 copy.33
  107.4 0.6 copy.32
  (73 shorter events, 5.5 us)
Async XLA Ops:
  0.6 18.9 %copy-start.1 = (bf16[256,2048]{1,0:T(8,128)(2,1)S(1)}, bf16[256,2048]{1,0:T(8,128)(2,1)}, u32[]{:S(2)}) copy-start(bf16[256,2048]{1,0:T(8,128)(2,1)} %da.1) | copy-start | bytes 3145732
  2.2 18.0 %copy-start = (bf16[256,2048]{1,0:T(8,128)(2,1)S(1)}, bf16[256,2048]{1,0:T(8,128)(2,1)}, u32[]{:S(2)}) copy-start(bf16[256,2048]{1,0:T(8,128)(2,1)} %qa.1) | copy-start | bytes 3145732
  2.9 25.5 %all-to-all-start.1 = ((bf16[64,8,256]{2,1,0:T(8,128)(2,1)}), bf16[64,8,256]{2,1,0:T(8,128)(2,1)S(1)}, u32[]{:S(2)}, u32[]{:S(2)}) async-start(bf16[64,8,256]{2,1,0:T(8,128)(2,1)} %bitcast.17), calls=%async_computation.1 | async-start | bytes 524288 | tf_op jit(solution)/shard_map/all_to_all | solution.py:148
  17.6 13.6 %collective-permute-start.7 = (bf16[256,128]{1,0:T(8,128)(2,1)}, bf16[256,128]{1,0:T(8,128)(2,1)S(1)}, u32[]{:S(2)}, u32[]{:S(2)}) collective-permute-start(bf16[256,128]{1,0:T(8,128)(2,1)} %constant_dynamic-slice_fusion), channel_id=1, source_target_pairs={{0,4},{4,0},{1,5},{5,1},{2,6},{6,2},{3,7},{7,3},{8,12},{12,8},{9,1... | collective-permute-start | bytes 196616 | tf_op jit(solution)/shard_map/ppermute | solution.py:149
  19.5 12.5 %collective-permute-start.6 = (bf16[256,128]{1,0:T(8,128)(2,1)}, bf16[256,128]{1,0:T(8,128)(2,1)S(1)}, u32[]{:S(2)}, u32[]{:S(2)}) collective-permute-start(bf16[256,128]{1,0:T(8,128)(2,1)} %constant_dynamic-slice_fusion.1), channel_id=1, source_target_pairs={{0,4},{4,0},{1,5},{5,1},{2,6},{6,2},{3,7},{7,3},{8,12},{12,8},{9,1... | collective-permute-start | bytes 196616 | tf_op jit(solution)/shard_map/ppermute | solution.py:149
  19.6 2.6 %copy-start.11 = (bf16[8,8192]{1,0:T(8,128)(2,1)S(1)}, bf16[8,8192]{1,0:T(8,128)(2,1)}, u32[]{:S(2)}) copy-start(bf16[8,8192]{1,0:T(8,128)(2,1)} %param.10) | copy-start | bytes 393220
  19.6 26.5 %collective-permute-start.2 = (bf16[256,1024]{1,0:T(8,128)(2,1)S(1)}, bf16[256,1024]{1,0:T(8,128)(2,1)S(1)}, u32[]{:S(2)}, u32[]{:S(2)}) collective-permute-start(bf16[256,1024]{1,0:T(8,128)(2,1)S(1)} %constant_dynamic-slice_fusion.2), channel_id=1, source_target_pairs={{0,4},{4,0},{1,5},{5,1},{2,6},{6,2},{3,7},{7,3},{8,12},{12,8},{9,1... | collective-permute-start | bytes 1572872 | tf_op jit(solution)/shard_map/ppermute | solution.py:149
  20.2 25.9 %collective-permute-start.1 = (bf16[256,1024]{1,0:T(8,128)(2,1)S(1)}, bf16[256,1024]{1,0:T(8,128)(2,1)S(1)}, u32[]{:S(2)}, u32[]{:S(2)}) collective-permute-start(bf16[256,1024]{1,0:T(8,128)(2,1)S(1)} %constant_dynamic-slice_fusion.3), channel_id=1, source_target_pairs={{0,4},{4,0},{1,5},{5,1},{2,6},{6,2},{3,7},{7,3},{8,12},{12,8},{9,1... | collective-permute-start | bytes 1572872 | tf_op jit(solution)/shard_map/ppermute | solution.py:149
  21.7 1.4 %collective-permute-start = (s32[2]{0:T(128)S(1)}, s32[2]{0:T(128)S(1)}, u32[]{:S(2)}, u32[]{:S(2)}) collective-permute-start(s32[2]{0:T(128)S(1)} %pad_add_fusion), channel_id=1, source_target_pairs={{0,4},{4,0},{1,5},{5,1},{2,6},{6,2},{3,7},{7,3},{8,12},{12,8},{9,1... | collective-permute-start | bytes 32 | tf_op jit(solution)/shard_map/ppermute | solution.py:149
  28.4 4.9 %copy-start.2 = (bf16[64,8,256]{2,1,0:T(8,128)(2,1)}, bf16[64,8,256]{2,1,0:T(8,128)(2,1)S(1)}, u32[]{:S(2)}) copy-start(bf16[64,8,256]{2,1,0:T(8,128)(2,1)S(1)} %all-to-all-done.1) | copy-start | bytes 786436
  28.4 17.7 %collective-permute-start.5 = (bf16[512,256]{1,0:T(8,128)(2,1)S(1)}, bf16[512,256]{1,0:T(8,128)(2,1)S(1)}, u32[]{:S(2)}, u32[]{:S(2)}) collective-permute-start(bf16[512,256]{1,0:T(8,128)(2,1)S(1)} %bitcast.44), channel_id=1, source_target_pairs={{0,128},{64,192},{128,0},{192,64},{1,129},{65,193},{129,1},{193,65... | collective-permute-start | bytes 786440 | tf_op jit(solution)/shard_map/ppermute | solution.py:150
  31.1 2.2 %copy-start.13 = (bf16[256,128]{1,0:T(8,128)(2,1)}, bf16[256,128]{1,0:T(8,128)(2,1)S(1)}, u32[]{:S(2)}) copy-start(bf16[256,128]{1,0:T(8,128)(2,1)S(1)} %collective-permute-done.7.vb) | copy-start | bytes 196612
  31.1 15.0 %collective-permute-start.4 = (bf16[512,256]{1,0:T(8,128)(2,1)S(1)}, bf16[512,256]{1,0:T(8,128)(2,1)S(1)}, u32[]{:S(2)}, u32[]{:S(2)}) collective-permute-start(bf16[512,256]{1,0:T(8,128)(2,1)S(1)} %bitcast.45), channel_id=1, source_target_pairs={{0,192},{64,0},{128,64},{192,128},{1,193},{65,1},{129,65},{193,129... | collective-permute-start | bytes 786440 | tf_op jit(solution)/shard_map/ppermute | solution.py:150
  32.0 1.3 %copy-start.14 = (bf16[256,128]{1,0:T(8,128)(2,1)}, bf16[256,128]{1,0:T(8,128)(2,1)S(1)}, u32[]{:S(2)}) copy-start(bf16[256,128]{1,0:T(8,128)(2,1)S(1)} %collective-permute-done.6.kb) | copy-start | bytes 196612
  32.0 14.2 %collective-permute-start.3 = (bf16[512,256]{1,0:T(8,128)(2,1)S(1)}, bf16[512,256]{1,0:T(8,128)(2,1)S(1)}, u32[]{:S(2)}, u32[]{:S(2)}) collective-permute-start(bf16[512,256]{1,0:T(8,128)(2,1)S(1)} %bitcast.46), channel_id=1, source_target_pairs={{0,64},{64,128},{128,192},{192,0},{1,65},{65,129},{129,193},{193,1... | collective-permute-start | bytes 786440 | tf_op jit(solution)/shard_map/ppermute | solution.py:150
  33.3 12.8 %all-to-all-start = ((bf16[8,8,2048]{2,1,0:T(8,128)(2,1)}), bf16[8,8,2048]{2,1,0:T(8,128)(2,1)S(1)}, u32[]{:S(2)}, u32[]{:S(2)}) async-start(bf16[8,8,2048]{2,1,0:T(8,128)(2,1)} %pad_maximum_fusion), calls=%async_computation | async-start | bytes 524288 | tf_op jit(solution)/shard_map/all_to_all | solution.py:148
  46.1 1.2 %copy-start.7 = (bf16[512,256]{1,0:T(8,128)(2,1)}, bf16[512,256]{1,0:T(8,128)(2,1)S(1)}, u32[]{:S(2)}) copy-start(bf16[512,256]{1,0:T(8,128)(2,1)S(1)} %collective-permute-done.4.s2) | copy-start | bytes 786436
  46.2 1.3 %copy-start.8 = (bf16[512,256]{1,0:T(8,128)(2,1)}, bf16[512,256]{1,0:T(8,128)(2,1)S(1)}, u32[]{:S(2)}) copy-start(bf16[512,256]{1,0:T(8,128)(2,1)S(1)} %collective-permute-done.3.s1) | copy-start | bytes 786436
  68.3 9.5 %collective-permute-start.8 = (bf16[256,256]{1,0:T(8,128)(2,1)}, bf16[256,256]{1,0:T(8,128)(2,1)S(1)}, u32[]{:S(2)}, u32[]{:S(2)}) collective-permute-start(bf16[256,256]{1,0:T(8,128)(2,1)} %get-tuple-element.25), channel_id=1, source_target_pairs={{0,4},{4,0},{1,5},{5,1},{2,6},{6,2},{3,7},{7,3},{8,12},{12,8},{9,1... | collective-permute-start | bytes 393224 | tf_op jit(solution)/shard_map/ppermute | solution.py:149
  68.8 14.7 %collective-permute-start.11 = (bf16[256,256]{1,0:T(8,128)(2,1)}, bf16[256,256]{1,0:T(8,128)(2,1)S(1)}, u32[]{:S(2)}, u32[]{:S(2)}) collective-permute-start(bf16[256,256]{1,0:T(8,128)(2,1)} %get-tuple-element.30), channel_id=1, source_target_pairs={{0,128},{64,192},{128,0},{192,64},{1,129},{65,193},{129,1},{193,65... | collective-permute-start | bytes 393224 | tf_op jit(solution)/shard_map/ppermute | solution.py:150
  71.0 11.6 %collective-permute-start.12 = (bf16[256,256]{1,0:T(8,128)(2,1)}, bf16[256,256]{1,0:T(8,128)(2,1)S(1)}, u32[]{:S(2)}, u32[]{:S(2)}) collective-permute-start(bf16[256,256]{1,0:T(8,128)(2,1)} %get-tuple-element.31), channel_id=1, source_target_pairs={{0,192},{64,0},{128,64},{192,128},{1,193},{65,1},{129,65},{193,129... | collective-permute-start | bytes 393224 | tf_op jit(solution)/shard_map/ppermute | solution.py:150
  75.1 12.7 %collective-permute-start.9 = (bf16[512,256]{1,0:T(8,128)(2,1)}, bf16[512,256]{1,0:T(8,128)(2,1)S(1)}, u32[]{:S(2)}, u32[]{:S(2)}) collective-permute-start(bf16[512,256]{1,0:T(8,128)(2,1)} %get-tuple-element.28), channel_id=1, source_target_pairs={{0,64},{64,128},{128,192},{192,0},{1,65},{65,129},{129,193},{193,1... | collective-permute-start | bytes 786440 | tf_op jit(solution)/shard_map/ppermute | solution.py:150
  75.1 12.7 %collective-permute-start.10 = (bf16[512,256]{1,0:T(8,128)(2,1)}, bf16[512,256]{1,0:T(8,128)(2,1)S(1)}, u32[]{:S(2)}, u32[]{:S(2)}) collective-permute-start(bf16[512,256]{1,0:T(8,128)(2,1)} %get-tuple-element.29), channel_id=1, source_target_pairs={{0,192},{64,0},{128,64},{192,128},{1,193},{65,1},{129,65},{193,129... | collective-permute-start | bytes 786440 | tf_op jit(solution)/shard_map/ppermute | solution.py:150
  77.8 18.7 %collective-permute-start.14 = (bf16[256,1024]{1,0:T(8,128)(2,1)}, bf16[256,1024]{1,0:T(8,128)(2,1)S(1)}, u32[]{:S(2)}, u32[]{:S(2)}) collective-permute-start(bf16[256,1024]{1,0:T(8,128)(2,1)} %get-tuple-element.35), channel_id=1, source_target_pairs={{0,4},{4,0},{1,5},{5,1},{2,6},{6,2},{3,7},{7,3},{8,12},{12,8},{9,1... | collective-permute-start | bytes 1572872 | tf_op jit(solution)/shard_map/ppermute | solution.py:149
  79.1 3.5 %copy-start.10 = (bf16[256,256]{1,0:T(8,128)(2,1)S(1)}, bf16[256,256]{1,0:T(8,128)(2,1)}, u32[]{:S(2)}) copy-start(bf16[256,256]{1,0:T(8,128)(2,1)} %get-tuple-element.38) | copy-start | bytes 393220
  79.1 10.0 %all-to-all-start.2 = ((bf16[8,8,2048]{2,1,0:T(8,128)(2,1)}), bf16[8,8,2048]{2,1,0:T(8,128)(2,1)S(1)}, u32[]{:S(2)}, u32[]{:S(2)}) async-start(bf16[8,8,2048]{2,1,0:T(8,128)(2,1)} %bitcast.54), calls=%async_computation.2 | async-start | bytes 524288 | tf_op jit(solution)/shard_map/all_to_all | solution.py:148
  82.7 5.1 %collective-permute-start.13 = (bf16[256,256]{1,0:T(8,128)(2,1)S(1)}, bf16[256,256]{1,0:T(8,128)(2,1)S(1)}, u32[]{:S(2)}, u32[]{:S(2)}) collective-permute-start(bf16[256,256]{1,0:T(8,128)(2,1)S(1)} %collective-permute-done.12), channel_id=1, source_target_pairs={{0,192},{64,0},{128,64},{192,128},{1,193},{65,1},{129,65},{193,129... | collective-permute-start | bytes 393224 | tf_op jit(solution)/shard_map/ppermute | solution.py:150
  82.8 5.0 %copy-start.9 = (bf16[512,256]{1,0:T(8,128)(2,1)S(1)}, bf16[512,256]{1,0:T(8,128)(2,1)}, u32[]{:S(2)}) copy-start(bf16[512,256]{1,0:T(8,128)(2,1)} %get-tuple-element.27) | copy-start | bytes 786436
  83.7 13.7 %collective-permute-start.15 = (bf16[256,1024]{1,0:T(8,128)(2,1)S(1)}, bf16[256,1024]{1,0:T(8,128)(2,1)S(1)}, u32[]{:S(2)}, u32[]{:S(2)}) collective-permute-start(bf16[256,1024]{1,0:T(8,128)(2,1)S(1)} %copy-done.17), channel_id=1, source_target_pairs={{0,4},{4,0},{1,5},{5,1},{2,6},{6,2},{3,7},{7,3},{8,12},{12,8},{9,1... | collective-permute-start | bytes 1572872 | tf_op jit(solution)/shard_map/ppermute | solution.py:149
  89.1 17.6 %all-to-all-start.3 = ((bf16[64,8,256]{2,1,0:T(8,128)(2,1)}), bf16[64,8,256]{2,1,0:T(8,128)(2,1)S(1)}, u32[]{:S(2)}, u32[]{:S(2)}) async-start(bf16[64,8,256]{2,1,0:T(8,128)(2,1)} %bitcast.26), calls=%async_computation.3 | async-start | bytes 524288 | tf_op jit(solution)/shard_map/all_to_all | solution.py:148
  95.2 2.2 %copy-start.15 = (bf16[256,2048]{1,0:T(8,128)(2,1)S(1)}, bf16[256,2048]{1,0:T(8,128)(2,1)}, u32[]{:S(2)}) copy-start(bf16[256,2048]{1,0:T(8,128)(2,1)} %get-tuple-element.36) | copy-start | bytes 3145732
  97.4 10.6 %copy-start.16 = (bf16[256,2048]{1,0:T(8,128)(2,1)}, bf16[256,2048]{1,0:T(8,128)(2,1)S(1)}, u32[]{:S(2)}) copy-start(bf16[256,2048]{1,0:T(8,128)(2,1)S(1)} %constant_dynamic-update-slice_fusion) | copy-start | bytes 3145732
  (6 other events, 5.7 us)

commit v3 on v2

--- a/solution.py
+++ b/solution.py
@@ -92,16 +92,20 @@
         @pl.when(jnp.logical_not(alive))
         def _():
             o_ref[...]=jnp.zeros_like(o_ref); g_ref[...]=jnp.zeros_like(g_ref)
-        @pl.when(alive)
-        def _():
+        def unit(seen):
             off,main=prompt(source)
             row=b*ROWS+lax.broadcasted_iota(jnp.int32,(M,1),0)%ROWS
-            vis=row>=lax.broadcasted_iota(jnp.int32,(M,SLOTS),1)
+            vis=row>=lax.broadcasted_iota(jnp.int32,(M,seen),1)
             live=(row<length).astype(F)
-            o,dq,g=pieces(stack(q_ref[...]),stack(d_ref[...]),[main+(None,),(ko[...],jnp.concatenate([vo[...],jnp.ones((SLOTS,HD),H)],axis=1),vis)],live)
+            val=jnp.concatenate([vo[:seen],jnp.ones((seen,HD),H)],axis=1)
+            o,dq,g=pieces(stack(q_ref[...]),stack(d_ref[...]),[main+(None,),(ko[:seen],val,vis)],live)
             o_ref[...]=unstack(o); g_ref[...]=unstack(dq)
             add(off,g[0])
-            okg[...]+=g[1][0]; ovg[...]+=g[1][1]
+            okg[:,:seen]+=g[1][0]; ovg[:,:seen]+=g[1][1]
+        @pl.when(jnp.logical_and(alive,b<2))
+        def _(): unit(SLOTS//2)
+        @pl.when(jnp.logical_and(alive,b>=2))
+        def _(): unit(SLOTS)
         @pl.when(b==3)
         def _():
             own_ref[:,:HD]=(okg[...]*SCALE).T.astype(H)
@@ -141,6 +145,16 @@
         compiler_params=pltpu.CompilerParams(vmem_limit_bytes=56*1024*1024),
         name="attn")(info,qa,da,qb,db,qd,*slabs,ka,va,kb,vb)
 
+def spread_kernel(k,v,out):
+    for core in range(2):
+        for head in range(4):
+            cols=pl.ds((2*head+core)*HD,HD)
+            piece=jnp.concatenate([k[:,cols],v[:,cols]],axis=1)
+            for z in range(8): out[z*8+core*4+head]=piece
+
+def spread(pk,pv):
+    return pl.pallas_call(spread_kernel,out_shape=jax.ShapeDtypeStruct((64,8,2*HD),H),name="spread")(pk,pv)
+
 ALL=("x","z","core","head")
 PLANE=("z","core","head")
 PAIR=("core","head")
@@ -155,9 +169,7 @@
 
 def shards(pq,pk,pv,pd,rq,rk,rv,rd,parent,lengths):
     x=lax.axis_index("x"); z=lax.axis_index("z"); core=lax.axis_index("core")
-    kv=jnp.concatenate([by_head(pk,HD),by_head(pv,HD)],axis=2)
-    kv=jnp.broadcast_to(kv[None],(8,8,8,2*HD)).reshape(64,8,2*HD)
-    slab=exchange(kv,PLANE).reshape(SLAB,2*HD)
+    slab=exchange(spread(pk,pv),PLANE).reshape(SLAB,2*HD)
     slabs=(slab,shift(slab,1),shift(slab,3),shift(slab,2))
     other=1-core
     far=lambda v,w: swap(lax.dynamic_slice_in_dim(v,other*w,w,1))

time: 110 us -> 110 us (level)
  Pallas kernels: 20.9 us -> 25.9 us
  local copies, waits for them, and re-layouts: 11.8 us -> 9.31 us
  waiting for transfers between devices: 23.1 us -> 21.6 us
    ppermute x8, starting transfers between devices: 13.3 us -> 9.28 us  [shift(): return lax.ppermute(v, 'x', [(i, (i + d) % 4) for i in range(4)])]
    all_to_all x4, starting transfers between devices: 28.2 us -> 31.8 us  [exchange(): return lax.all_to_all(v, axes, split_axis=0, concat_axis=0, tiled=True)]
    pallas_call x1, Pallas kernels: 20.9 us -> 24.3 us  [call(): pl.pallas_call(kernel, grid_spec=pltpu.PrefetchScalarGridSpec(num_scalar_...]
    pallas_call x0 -> x1, Pallas kernels: none -> 1.6 us  [spread(): pl.pallas_call(spread_kernel, out_shape=jax.ShapeDtypeStruct((64, 8, 2 *...]
    transpose x4 -> x2, local copies, waits for them, and re-layouts: 1.55 us -> 0.02 us  [by_head(): return v.reshape(8, 4, 2, width).transpose(2, 1, 0, 3).reshape(8, 8, width)]
  transfers between devices with their start and end apart: 20 -> 20, of which waited for: 5 -> 4; matrix products, arithmetic and copies ran while one was open for 10% -> 10% of each run, Pallas kernels for 0% -> 0%
where the time goes in v3:
time: 110 us; the launch traced here: 109 us
  starting transfers between devices  44.7 us (41%)
  Pallas kernels  25.9 us (24%)
  waiting for transfers between devices  21.6 us (20%)
  local copies, waits for them, and re-layouts  9.31 us (8%)
  other arithmetic  4.87 us (4%)
  between operations  2.2 us (2%)
    all_to_all x4, starting transfers between devices, exchange(): return lax.all_to_all(v, axes, split_axis=0, concat_axis=0, tiled=True)  31.8 us
    pallas_call x1, Pallas kernels, call(): pl.pallas_call(kernel, grid_spec=pltpu.PrefetchScalarGridSpec(num_scalar_...  24.3 us
    all_to_all x4, waiting for transfers between devices, exchange(): return lax.all_to_all(v, axes, split_axis=0, concat_axis=0, tiled=True)  18.8 us
    ppermute x8, starting transfers between devices, shift(): return lax.ppermute(v, 'x', [(i, (i + d) % 4) for i in range(4)])  9.28 us
    ppermute x8, starting transfers between devices, swap(): return lax.ppermute(v, 'core', [(0, 1), (1, 0)])  3.64 us
    dynamic_slice x4, local copies, waits for them, and re-layouts, shards(): far = lambda v, w: swap(lax.dynamic_slice_in_dim(v, other * w, w, 1))  3.03 us
    ppermute x8, waiting for transfers between devices, shift(): return lax.ppermute(v, 'x', [(i, (i + d) % 4) for i in range(4)])  2.77 us
  transfers between devices with their start and end apart: 20, of which 4 were waited for; matrix products, arithmetic and copies ran while one was open for 10% of the time, Pallas kernels for 0%

profile of v3, /device:TPU:1, one launch (start us, length us, event | category | flops | bytes accessed | tf_op | source)
XLA Modules:
  0.0 108.6 jit_solution(2694742136268065312)
XLA Ops:
  0.7 1.6 %spread.1 = bf16[64,8,256]{2,1,0:T(8,128)(2,1)} custom-call(bf16[8,1024]{1,0:T(8,128)(2,1)} %k.1, bf16[8,1024]{1,0:T(8,128)(2,1)} %v.1), custom_call_target="tpu_custom_call" | custom-call | tf_op jit(solution)/shard_map/spread/pallas_call | solution.py:156
  2.3 13.2 %all-to-all-start.1 = ((bf16[64,8,256]{2,1,0:T(8,128)(2,1)}), bf16[64,8,256]{2,1,0:T(8,128)(2,1)S(1)}, u32[]{:S(2)}, u32[]{:S(2)}) async-start(bf16[64,8,256]{2,1,0:T(8,128)(2,1)} %spread.1), calls=%async_computation.1 | async-start | bytes 524288 | tf_op jit(solution)/shard_map/all_to_all | solution.py:162
  15.4 1.5 %constant_dynamic-slice_fusion = bf16[256,128]{1,0:T(8,128)(2,1)} fusion(bf16[256,256]{1,0:T(8,128)(2,1)} %va.1, s32[]{:T(128)S(6)} %select_n.62), kind=kLoop, calls=%fused_computation.16 | loop fusion | bytes 131076 | tf_op jit(solution)/shard_map/dynamic_slice | solution.py:175
  17.4 1.5 %constant_dynamic-slice_fusion.1 = bf16[256,128]{1,0:T(8,128)(2,1)} fusion(bf16[256,256]{1,0:T(8,128)(2,1)} %ka.1, s32[]{:T(128)S(6)} %select_n.62), kind=kLoop, calls=%fused_computation.17 | loop fusion | bytes 131076 | tf_op jit(solution)/shard_map/dynamic_slice | solution.py:175
  21.6 0.9 copy-done.12
  22.5 5.2 %all-to-all-done.1 = bf16[64,8,256]{2,1,0:T(8,128)(2,1)S(1)} async-done(((bf16[64,8,256]{2,1,0:T(8,128)(2,1)}), bf16[64,8,256]{2,1,0:T(8,128)(2,1)S(1)}, u32[]{:S(2)}, u32[]{:S(2)}) %all-to-all-start.1) | async-done | bytes 262176 | tf_op jit(solution)/shard_map/all_to_all | solution.py:162
  27.7 2.7 %collective-permute-start.5 = (bf16[512,256]{1,0:T(8,128)(2,1)S(1)}, bf16[512,256]{1,0:T(8,128)(2,1)S(1)}, u32[]{:S(2)}, u32[]{:S(2)}) collective-permute-start(bf16[512,256]{1,0:T(8,128)(2,1)S(1)} %bitcast.35), channel_id=1, source_target_pairs={{0,128},{64,192},{128,0},{192,64},{1,129},{65,193},{129,1},{193,65... | collective-permute-start | bytes 786440 | tf_op jit(solution)/shard_map/ppermute | solution.py:164
  30.5 0.9 collective-permute-start.4
  31.3 0.6 collective-permute-start.3
  31.9 0.7 pad_maximum_fusion
  32.7 6.2 %all-to-all-start = ((bf16[8,8,2048]{2,1,0:T(8,128)(2,1)}), bf16[8,8,2048]{2,1,0:T(8,128)(2,1)S(1)}, u32[]{:S(2)}, u32[]{:S(2)}) async-start(bf16[8,8,2048]{2,1,0:T(8,128)(2,1)} %pad_maximum_fusion), calls=%async_computation | async-start | bytes 524288 | tf_op jit(solution)/shard_map/all_to_all | solution.py:162
  38.9 0.6 fusion.4
  39.5 1.8 %compare_select_fusion.7.info = s32[8]{0:T(128)} fusion(s32[]{:T(128)} %bitcast.33, s32[]{:T(128)} %bitcast.2, s32[]{:T(128)} %bitcast.34, s32[]{:T(128)} %bitcast, s32[]{:T(128)S(6)} %axis_index.41, s32[]{:T(128)S(6)} %select_n.52, s32[]{:T(128)S(6)} %sub.11, s32[]{:T(128)S(6)} %axis_index.35), kind=kLoop, calls=%fused_computation.13 | loop fusion | flops 128 | bytes 64 | tf_op jit(solution)/shard_map/jit(_where)/select_n | solution.py:185
  41.3 4.2 %all-to-all-done = bf16[8,8,2048]{2,1,0:T(8,128)(2,1)S(1)} async-done(((bf16[8,8,2048]{2,1,0:T(8,128)(2,1)}), bf16[8,8,2048]{2,1,0:T(8,128)(2,1)S(1)}, u32[]{:S(2)}, u32[]{:S(2)}) %all-to-all-start) | async-done | bytes 262176 | tf_op jit(solution)/shard_map/all_to_all | solution.py:162
  45.5 0.6 copy-done.3
  46.8 24.3 %attn.1 = (bf16[256,2048]{1,0:T(8,128)(2,1)}, bf16[256,2048]{1,0:T(8,128)(2,1)}, bf16[256,1024]{1,0:T(8,128)(2,1)}, bf16[256,1024]{1,0:T(8,128)(2,1)}, bf16[64,2...) custom-call(s32[8]{0:T(128)} %compare_select_fusion.7.info, ...), custom_call_target="tpu_custom_call" | custom-call | tf_op jit(solution)/shard_map/attn/pallas_call | solution.py:139
  71.6 1.5 %collective-permute-start.9 = (bf16[512,256]{1,0:T(8,128)(2,1)}, bf16[512,256]{1,0:T(8,128)(2,1)S(1)}, u32[]{:S(2)}, u32[]{:S(2)}) collective-permute-start(bf16[512,256]{1,0:T(8,128)(2,1)} %get-tuple-element.28), channel_id=1, source_target_pairs={{0,64},{64,128},{128,192},{192,0},{1,65},{65,129},{129,193},{193,1... | collective-permute-start | bytes 786440 | tf_op jit(solution)/shard_map/ppermute | solution.py:164
  73.1 1.7 %collective-permute-start.10 = (bf16[512,256]{1,0:T(8,128)(2,1)}, bf16[512,256]{1,0:T(8,128)(2,1)S(1)}, u32[]{:S(2)}, u32[]{:S(2)}) collective-permute-start(bf16[512,256]{1,0:T(8,128)(2,1)} %get-tuple-element.29), channel_id=1, source_target_pairs={{0,192},{64,0},{128,64},{192,128},{1,193},{65,1},{129,65},{193,129... | collective-permute-start | bytes 786440 | tf_op jit(solution)/shard_map/ppermute | solution.py:164
  74.8 1.2 %collective-permute-start.14 = (bf16[256,1024]{1,0:T(8,128)(2,1)}, bf16[256,1024]{1,0:T(8,128)(2,1)S(1)}, u32[]{:S(2)}, u32[]{:S(2)}) collective-permute-start(bf16[256,1024]{1,0:T(8,128)(2,1)} %get-tuple-element.35), channel_id=1, source_target_pairs={{0,4},{4,0},{1,5},{5,1},{2,6},{6,2},{3,7},{7,3},{8,12},{12,8},{9,1... | collective-permute-start | bytes 1572872 | tf_op jit(solution)/shard_map/ppermute | solution.py:163
  76.0 3.5 %all-to-all-start.2 = ((bf16[8,8,2048]{2,1,0:T(8,128)(2,1)}), bf16[8,8,2048]{2,1,0:T(8,128)(2,1)S(1)}, u32[]{:S(2)}, u32[]{:S(2)}) async-start(bf16[8,8,2048]{2,1,0:T(8,128)(2,1)} %bitcast.45), calls=%async_computation.2 | async-start | bytes 524288 | tf_op jit(solution)/shard_map/all_to_all | solution.py:162
  79.5 1.8 %collective-permute-start.13 = (bf16[256,256]{1,0:T(8,128)(2,1)S(1)}, bf16[256,256]{1,0:T(8,128)(2,1)S(1)}, u32[]{:S(2)}, u32[]{:S(2)}) collective-permute-start(bf16[256,256]{1,0:T(8,128)(2,1)S(1)} %collective-permute-done.12), channel_id=1, source_target_pairs={{0,192},{64,0},{128,64},{192,128},{1,193},{65,1},{129,65},{193,129... | collective-permute-start | bytes 393224 | tf_op jit(solution)/shard_map/ppermute | solution.py:164
  81.4 0.7 pad_maximum_fusion.2
  82.5 2.8 %collective-permute-done.13 = bf16[256,256]{1,0:T(8,128)(2,1)S(1)} collective-permute-done((bf16[256,256]{1,0:T(8,128)(2,1)S(1)}, bf16[256,256]{1,0:T(8,128)(2,1)S(1)}, u32[]{:S(2)}, u32[]{:S(2)}) %collective-permute-start.13) | collective-permute-done | bytes 131104 | tf_op jit(solution)/shard_map/ppermute | solution.py:164
  85.2 0.8 add_convert_fusion
  86.1 9.0 %all-to-all-start.3 = ((bf16[64,8,256]{2,1,0:T(8,128)(2,1)}), bf16[64,8,256]{2,1,0:T(8,128)(2,1)S(1)}, u32[]{:S(2)}, u32[]{:S(2)}) async-start(bf16[64,8,256]{2,1,0:T(8,128)(2,1)} %bitcast.19), calls=%async_computation.3 | async-start | bytes 524288 | tf_op jit(solution)/shard_map/all_to_all | solution.py:162
  95.0 0.7 pad_maximum_fusion.1
  95.7 0.7 copy.29
  96.4 0.7 copy.28
  97.1 0.8 constant_dynamic-update-slice_fusion.1
  98.0 9.4 %all-to-all-done.3 = bf16[64,8,256]{2,1,0:T(8,128)(2,1)S(1)} async-done(((bf16[64,8,256]{2,1,0:T(8,128)(2,1)}), bf16[64,8,256]{2,1,0:T(8,128)(2,1)S(1)}, u32[]{:S(2)}, u32[]{:S(2)}) %all-to-all-start.3) | async-done | bytes 262176 | tf_op jit(solution)/shard_map/all_to_all | solution.py:162
  107.4 0.6 copy.31
  108.0 0.6 copy.30
  (70 shorter events, 3.6 us)
Async XLA Ops:
  0.6 18.3 %copy-start.1 = (bf16[256,2048]{1,0:T(8,128)(2,1)S(1)}, bf16[256,2048]{1,0:T(8,128)(2,1)}, u32[]{:S(2)}) copy-start(bf16[256,2048]{1,0:T(8,128)(2,1)} %da.1) | copy-start | bytes 3145732
  0.6 18.9 %copy-start = (bf16[256,2048]{1,0:T(8,128)(2,1)S(1)}, bf16[256,2048]{1,0:T(8,128)(2,1)}, u32[]{:S(2)}) copy-start(bf16[256,2048]{1,0:T(8,128)(2,1)} %qa.1) | copy-start | bytes 3145732
  2.3 25.5 %all-to-all-start.1 = ((bf16[64,8,256]{2,1,0:T(8,128)(2,1)}), bf16[64,8,256]{2,1,0:T(8,128)(2,1)S(1)}, u32[]{:S(2)}, u32[]{:S(2)}) async-start(bf16[64,8,256]{2,1,0:T(8,128)(2,1)} %spread.1), calls=%async_computation.1 | async-start | bytes 524288 | tf_op jit(solution)/shard_map/all_to_all | solution.py:162
  16.9 13.6 %collective-permute-start.7 = (bf16[256,128]{1,0:T(8,128)(2,1)}, bf16[256,128]{1,0:T(8,128)(2,1)S(1)}, u32[]{:S(2)}, u32[]{:S(2)}) collective-permute-start(bf16[256,128]{1,0:T(8,128)(2,1)} %constant_dynamic-slice_fusion), channel_id=1, source_target_pairs={{0,4},{4,0},{1,5},{5,1},{2,6},{6,2},{3,7},{7,3},{8,12},{12,8},{9,1... | collective-permute-start | bytes 196616 | tf_op jit(solution)/shard_map/ppermute | solution.py:163
  18.8 12.5 %collective-permute-start.6 = (bf16[256,128]{1,0:T(8,128)(2,1)}, bf16[256,128]{1,0:T(8,128)(2,1)S(1)}, u32[]{:S(2)}, u32[]{:S(2)}) collective-permute-start(bf16[256,128]{1,0:T(8,128)(2,1)} %constant_dynamic-slice_fusion.1), channel_id=1, source_target_pairs={{0,4},{4,0},{1,5},{5,1},{2,6},{6,2},{3,7},{7,3},{8,12},{12,8},{9,1... | collective-permute-start | bytes 196616 | tf_op jit(solution)/shard_map/ppermute | solution.py:163
  18.9 2.6 %copy-start.11 = (bf16[8,8192]{1,0:T(8,128)(2,1)S(1)}, bf16[8,8192]{1,0:T(8,128)(2,1)}, u32[]{:S(2)}) copy-start(bf16[8,8192]{1,0:T(8,128)(2,1)} %param.10) | copy-start | bytes 393220
  19.0 26.5 %collective-permute-start.2 = (bf16[256,1024]{1,0:T(8,128)(2,1)S(1)}, bf16[256,1024]{1,0:T(8,128)(2,1)S(1)}, u32[]{:S(2)}, u32[]{:S(2)}) collective-permute-start(bf16[256,1024]{1,0:T(8,128)(2,1)S(1)} %constant_dynamic-slice_fusion.2), channel_id=1, source_target_pairs={{0,4},{4,0},{1,5},{5,1},{2,6},{6,2},{3,7},{7,3},{8,12},{12,8},{9,1... | collective-permute-start | bytes 1572872 | tf_op jit(solution)/shard_map/ppermute | solution.py:163
  19.5 25.9 %collective-permute-start.1 = (bf16[256,1024]{1,0:T(8,128)(2,1)S(1)}, bf16[256,1024]{1,0:T(8,128)(2,1)S(1)}, u32[]{:S(2)}, u32[]{:S(2)}) collective-permute-start(bf16[256,1024]{1,0:T(8,128)(2,1)S(1)} %constant_dynamic-slice_fusion.3), channel_id=1, source_target_pairs={{0,4},{4,0},{1,5},{5,1},{2,6},{6,2},{3,7},{7,3},{8,12},{12,8},{9,1... | collective-permute-start | bytes 1572872 | tf_op jit(solution)/shard_map/ppermute | solution.py:163
  21.1 1.4 %collective-permute-start = (s32[2]{0:T(128)S(1)}, s32[2]{0:T(128)S(1)}, u32[]{:S(2)}, u32[]{:S(2)}) collective-permute-start(s32[2]{0:T(128)S(1)} %pad_add_fusion), channel_id=1, source_target_pairs={{0,4},{4,0},{1,5},{5,1},{2,6},{6,2},{3,7},{7,3},{8,12},{12,8},{9,1... | collective-permute-start | bytes 32 | tf_op jit(solution)/shard_map/ppermute | solution.py:163
  27.7 4.9 %copy-start.2 = (bf16[64,8,256]{2,1,0:T(8,128)(2,1)}, bf16[64,8,256]{2,1,0:T(8,128)(2,1)S(1)}, u32[]{:S(2)}) copy-start(bf16[64,8,256]{2,1,0:T(8,128)(2,1)S(1)} %all-to-all-done.1) | copy-start | bytes 786436
  27.7 17.7 %collective-permute-start.5 = (bf16[512,256]{1,0:T(8,128)(2,1)S(1)}, bf16[512,256]{1,0:T(8,128)(2,1)S(1)}, u32[]{:S(2)}, u32[]{:S(2)}) collective-permute-start(bf16[512,256]{1,0:T(8,128)(2,1)S(1)} %bitcast.35), channel_id=1, source_target_pairs={{0,128},{64,192},{128,0},{192,64},{1,129},{65,193},{129,1},{193,65... | collective-permute-start | bytes 786440 | tf_op jit(solution)/shard_map/ppermute | solution.py:164
  30.5 2.2 %copy-start.13 = (bf16[256,128]{1,0:T(8,128)(2,1)}, bf16[256,128]{1,0:T(8,128)(2,1)S(1)}, u32[]{:S(2)}) copy-start(bf16[256,128]{1,0:T(8,128)(2,1)S(1)} %collective-permute-done.7.vb) | copy-start | bytes 196612
  30.5 15.0 %collective-permute-start.4 = (bf16[512,256]{1,0:T(8,128)(2,1)S(1)}, bf16[512,256]{1,0:T(8,128)(2,1)S(1)}, u32[]{:S(2)}, u32[]{:S(2)}) collective-permute-start(bf16[512,256]{1,0:T(8,128)(2,1)S(1)} %bitcast.36), channel_id=1, source_target_pairs={{0,192},{64,0},{128,64},{192,128},{1,193},{65,1},{129,65},{193,129... | collective-permute-start | bytes 786440 | tf_op jit(solution)/shard_map/ppermute | solution.py:164
  31.3 1.3 %copy-start.14 = (bf16[256,128]{1,0:T(8,128)(2,1)}, bf16[256,128]{1,0:T(8,128)(2,1)S(1)}, u32[]{:S(2)}) copy-start(bf16[256,128]{1,0:T(8,128)(2,1)S(1)} %collective-permute-done.6.kb) | copy-start | bytes 196612
  31.3 14.2 %collective-permute-start.3 = (bf16[512,256]{1,0:T(8,128)(2,1)S(1)}, bf16[512,256]{1,0:T(8,128)(2,1)S(1)}, u32[]{:S(2)}, u32[]{:S(2)}) collective-permute-start(bf16[512,256]{1,0:T(8,128)(2,1)S(1)} %bitcast.37), channel_id=1, source_target_pairs={{0,64},{64,128},{128,192},{192,0},{1,65},{65,129},{129,193},{193,1... | collective-permute-start | bytes 786440 | tf_op jit(solution)/shard_map/ppermute | solution.py:164
  32.7 12.8 %all-to-all-start = ((bf16[8,8,2048]{2,1,0:T(8,128)(2,1)}), bf16[8,8,2048]{2,1,0:T(8,128)(2,1)S(1)}, u32[]{:S(2)}, u32[]{:S(2)}) async-start(bf16[8,8,2048]{2,1,0:T(8,128)(2,1)} %pad_maximum_fusion), calls=%async_computation | async-start | bytes 524288 | tf_op jit(solution)/shard_map/all_to_all | solution.py:162
  45.5 1.3 %copy-start.8 = (bf16[512,256]{1,0:T(8,128)(2,1)}, bf16[512,256]{1,0:T(8,128)(2,1)S(1)}, u32[]{:S(2)}) copy-start(bf16[512,256]{1,0:T(8,128)(2,1)S(1)} %collective-permute-done.3.s1) | copy-start | bytes 786436
  71.1 3.7 %collective-permute-start.8 = (bf16[256,256]{1,0:T(8,128)(2,1)}, bf16[256,256]{1,0:T(8,128)(2,1)S(1)}, u32[]{:S(2)}, u32[]{:S(2)}) collective-permute-start(bf16[256,256]{1,0:T(8,128)(2,1)} %get-tuple-element.25), channel_id=1, source_target_pairs={{0,4},{4,0},{1,5},{5,1},{2,6},{6,2},{3,7},{7,3},{8,12},{12,8},{9,1... | collective-permute-start | bytes 393224 | tf_op jit(solution)/shard_map/ppermute | solution.py:163
  71.6 10.5 %collective-permute-start.11 = (bf16[256,256]{1,0:T(8,128)(2,1)}, bf16[256,256]{1,0:T(8,128)(2,1)S(1)}, u32[]{:S(2)}, u32[]{:S(2)}) collective-permute-start(bf16[256,256]{1,0:T(8,128)(2,1)} %get-tuple-element.30), channel_id=1, source_target_pairs={{0,128},{64,192},{128,0},{192,64},{1,129},{65,193},{129,1},{193,65... | collective-permute-start | bytes 393224 | tf_op jit(solution)/shard_map/ppermute | solution.py:164
  71.6 8.0 %collective-permute-start.12 = (bf16[256,256]{1,0:T(8,128)(2,1)}, bf16[256,256]{1,0:T(8,128)(2,1)S(1)}, u32[]{:S(2)}, u32[]{:S(2)}) collective-permute-start(bf16[256,256]{1,0:T(8,128)(2,1)} %get-tuple-element.31), channel_id=1, source_target_pairs={{0,192},{64,0},{128,64},{192,128},{1,193},{65,1},{129,65},{193,129... | collective-permute-start | bytes 393224 | tf_op jit(solution)/shard_map/ppermute | solution.py:164
  71.6 13.6 %collective-permute-start.9 = (bf16[512,256]{1,0:T(8,128)(2,1)}, bf16[512,256]{1,0:T(8,128)(2,1)S(1)}, u32[]{:S(2)}, u32[]{:S(2)}) collective-permute-start(bf16[512,256]{1,0:T(8,128)(2,1)} %get-tuple-element.28), channel_id=1, source_target_pairs={{0,64},{64,128},{128,192},{192,0},{1,65},{65,129},{129,193},{193,1... | collective-permute-start | bytes 786440 | tf_op jit(solution)/shard_map/ppermute | solution.py:164
  73.1 12.1 %collective-permute-start.10 = (bf16[512,256]{1,0:T(8,128)(2,1)}, bf16[512,256]{1,0:T(8,128)(2,1)S(1)}, u32[]{:S(2)}, u32[]{:S(2)}) collective-permute-start(bf16[512,256]{1,0:T(8,128)(2,1)} %get-tuple-element.29), channel_id=1, source_target_pairs={{0,192},{64,0},{128,64},{192,128},{1,193},{65,1},{129,65},{193,129... | collective-permute-start | bytes 786440 | tf_op jit(solution)/shard_map/ppermute | solution.py:164
  74.8 22.2 %collective-permute-start.14 = (bf16[256,1024]{1,0:T(8,128)(2,1)}, bf16[256,1024]{1,0:T(8,128)(2,1)S(1)}, u32[]{:S(2)}, u32[]{:S(2)}) collective-permute-start(bf16[256,1024]{1,0:T(8,128)(2,1)} %get-tuple-element.35), channel_id=1, source_target_pairs={{0,4},{4,0},{1,5},{5,1},{2,6},{6,2},{3,7},{7,3},{8,12},{12,8},{9,1... | collective-permute-start | bytes 1572872 | tf_op jit(solution)/shard_map/ppermute | solution.py:163
  76.0 3.5 %copy-start.10 = (bf16[256,256]{1,0:T(8,128)(2,1)S(1)}, bf16[256,256]{1,0:T(8,128)(2,1)}, u32[]{:S(2)}) copy-start(bf16[256,256]{1,0:T(8,128)(2,1)} %get-tuple-element.38) | copy-start | bytes 393220
  76.0 10.1 %all-to-all-start.2 = ((bf16[8,8,2048]{2,1,0:T(8,128)(2,1)}), bf16[8,8,2048]{2,1,0:T(8,128)(2,1)S(1)}, u32[]{:S(2)}, u32[]{:S(2)}) async-start(bf16[8,8,2048]{2,1,0:T(8,128)(2,1)} %bitcast.45), calls=%async_computation.2 | async-start | bytes 524288 | tf_op jit(solution)/shard_map/all_to_all | solution.py:162
  79.5 2.6 %copy-start.17 = (bf16[256,1024]{1,0:T(8,128)(2,1)S(1)}, bf16[256,1024]{1,0:T(8,128)(2,1)}, u32[]{:S(2)}) copy-start(bf16[256,1024]{1,0:T(8,128)(2,1)} %get-tuple-element.37) | copy-start | bytes 1572868
  79.5 5.7 %collective-permute-start.13 = (bf16[256,256]{1,0:T(8,128)(2,1)S(1)}, bf16[256,256]{1,0:T(8,128)(2,1)S(1)}, u32[]{:S(2)}, u32[]{:S(2)}) collective-permute-start(bf16[256,256]{1,0:T(8,128)(2,1)S(1)} %collective-permute-done.12), channel_id=1, source_target_pairs={{0,192},{64,0},{128,64},{192,128},{1,193},{65,1},{129,65},{193,129... | collective-permute-start | bytes 393224 | tf_op jit(solution)/shard_map/ppermute | solution.py:164
  81.4 3.8 %copy-start.9 = (bf16[512,256]{1,0:T(8,128)(2,1)S(1)}, bf16[512,256]{1,0:T(8,128)(2,1)}, u32[]{:S(2)}) copy-start(bf16[512,256]{1,0:T(8,128)(2,1)} %get-tuple-element.27) | copy-start | bytes 786436
  82.1 15.8 %collective-permute-start.15 = (bf16[256,1024]{1,0:T(8,128)(2,1)S(1)}, bf16[256,1024]{1,0:T(8,128)(2,1)S(1)}, u32[]{:S(2)}, u32[]{:S(2)}) collective-permute-start(bf16[256,1024]{1,0:T(8,128)(2,1)S(1)} %copy-done.17), channel_id=1, source_target_pairs={{0,4},{4,0},{1,5},{5,1},{2,6},{6,2},{3,7},{7,3},{8,12},{12,8},{9,1... | collective-permute-start | bytes 1572872 | tf_op jit(solution)/shard_map/ppermute | solution.py:163
  86.1 21.3 %all-to-all-start.3 = ((bf16[64,8,256]{2,1,0:T(8,128)(2,1)}), bf16[64,8,256]{2,1,0:T(8,128)(2,1)S(1)}, u32[]{:S(2)}, u32[]{:S(2)}) async-start(bf16[64,8,256]{2,1,0:T(8,128)(2,1)} %bitcast.19), calls=%async_computation.3 | async-start | bytes 524288 | tf_op jit(solution)/shard_map/all_to_all | solution.py:162
  95.7 2.2 %copy-start.15 = (bf16[256,2048]{1,0:T(8,128)(2,1)S(1)}, bf16[256,2048]{1,0:T(8,128)(2,1)}, u32[]{:S(2)}) copy-start(bf16[256,2048]{1,0:T(8,128)(2,1)} %get-tuple-element.36) | copy-start | bytes 3145732
  97.9 10.6 %copy-start.16 = (bf16[256,2048]{1,0:T(8,128)(2,1)}, bf16[256,2048]{1,0:T(8,128)(2,1)S(1)}, u32[]{:S(2)}) copy-start(bf16[256,2048]{1,0:T(8,128)(2,1)S(1)} %constant_dynamic-update-slice_fusion) | copy-start | bytes 3145732
  (6 other events, 5.9 us)
